TPU v7x, 32 devices: a whole 2x2x4 slice. The times are simulated.
32 devices in a mesh: grp: 2 (over y), seq: 16 (over z, x, core).
Axes of the slice: x: 2, y: 2, z: 4, core: 2. Of those that a mesh axis runs over, the one named last changes fastest.
Arguments:
- queries: bfloat16 [4096, 768], P(('grp', 'seq')), parts along dimension 0, may hold values from -2.5 to 2.5
- key_rows: bfloat16 [4096, 768], P(('grp', 'seq')), parts along dimension 0, may hold values from -2.5 to 2.5
- value_rows: bfloat16 [4096, 768], P(('grp', 'seq')), parts along dimension 0, may hold values from -6 to 6
- out_grad: bfloat16 [4096, 768], P(('grp', 'seq')), parts along dimension 0, may hold values from -6 to 6
- ssm_input: bfloat16 [4096, 768], P(('grp', 'seq')), parts along dimension 0, may hold values from -0.125 to 0.125
- state_write: bfloat16 [4096, 128], P(('grp', 'seq')), parts along dimension 0, may hold values from -0.1875 to 0.1875
- state_read: bfloat16 [4096, 128], P(('grp', 'seq')), parts along dimension 0, may hold values from -0.1875 to 0.1875
- log_decay: float32 [12, 4096], P(None, ('grp', 'seq')), parts along dimension 1, may hold values from -0.8 to 0, as said below
- block_lists: int32 [32, 4], P(('grp', 'seq')), parts along dimension 0, may hold values from -1 to 15, as said below
- rec_lengths: int32 [16], P('grp'), parts along dimension 0, may hold values from 1 to 1024, 2048 in all
Outputs:
- grad_queries: bfloat16 [4096, 768], P(('grp', 'seq')), parts along dimension 0
- grad_keys: bfloat16 [4096, 768], P(('grp', 'seq')), parts along dimension 0
- grad_values: bfloat16 [4096, 768], P(('grp', 'seq')), parts along dimension 0
- grad_input: bfloat16 [4096, 768], P(('grp', 'seq')), parts along dimension 0
- grad_write: bfloat16 [4096, 128], P(('grp', 'seq')), parts along dimension 0
- grad_read: bfloat16 [4096, 128], P(('grp', 'seq')), parts along dimension 0
- grad_decay: float32 [12, 4096], P(None, ('grp', 'seq')), parts along dimension 1
There are 2 independent parts, one for each index of `grp`. A program takes and returns all parts, laid end to end along the dimension named above; each array names one. Nothing has to cross between parts.
Inputs may be any that keep to these rules, and one draw needn't show every extreme that they name: `block_lists`: entry 0 of row b is b itself; the other 3 entries are distinct blocks 1 to 4 blocks before b, each replaced by -1 where it would be negative. `log_decay`: all log-decays are negative.
All inputs are finite; a program needn't handle non-finite values.
Results may differ from a plain program's by a relative error of at most 0.0057.
Values may be sent and summed in bfloat16 or wider, within the bound.
A program may use at most 256 MiB of HBM per device.

v0:
```python
import jax
import jax.numpy as jnp
from jax import lax
from jax.sharding import PartitionSpec as P

KWIN = 4


PRECISE = lax.Precision.HIGHEST


def passed_along(block, axis, distance):
    devices = range(lax.axis_size(axis))
    route = [(i - distance, i) for i in devices if i - distance in devices]
    return lax.ppermute(block, axis, route)


def carried_in(part, axis, combine, identity, reverse):
    count = lax.axis_size(axis)
    place = lax.axis_index(axis)
    ahead = count - 1 - place if reverse else place
    gathered = jax.tree.map(lambda a: lax.all_gather(a, axis), part)
    state = jax.tree.map(lambda a, e: jnp.zeros_like(a) + jnp.asarray(e, a.dtype), part, identity)

    def one(hop, state):
        source = count - 1 - hop if reverse else hop
        return combine(
            state, jax.tree.map(lambda a: lax.dynamic_index_in_dim(a, source, 0, False), gathered)
        )

    return lax.fori_loop(0, ahead, one, state)


def recording_of(positions, rec_lengths):
    boundary = jnp.cumsum(rec_lengths)
    return jnp.sum((positions[..., None] >= boundary).astype(jnp.int32), axis=-1)


def keep_of(positions, rec_lengths):
    boundary = jnp.cumsum(rec_lengths)
    opening = jnp.any(positions[..., None] == boundary, axis=-1) | (positions == 0)
    return jnp.where(opening, 0.0, 1.0).astype(jnp.float32)


def piece_setup(decay_part, keep_part, rec_part):
    span_len = decay_part.shape[-1]
    upper_tri = jnp.arange(span_len)[:, None] >= jnp.arange(span_len)[None, :]
    cumulative = jnp.cumsum(decay_part, axis=-1)
    spread = cumulative[..., :, None] - cumulative[..., None, :]
    same_rec = rec_part[:, :, None] == rec_part[:, None, :]
    live_pair = (upper_tri[None] & same_rec)[:, None]
    lower_mat = jnp.where(live_pair, jnp.exp(jnp.where(live_pair, spread, 0.0)), 0.0)
    head_live = keep_part[:, :1] * (rec_part == rec_part[:, :1]).astype(jnp.float32)
    enter_w = jnp.exp(cumulative) * head_live[:, None, :]
    tail_live = (rec_part == rec_part[:, -1:]).astype(jnp.float32)
    leave_w = jnp.exp(cumulative[..., -1:] - cumulative) * tail_live[:, None, :]
    return (lower_mat, enter_w, leave_w)


def piece_summary(input_part, write_part, read_part, grad_part, enter_w, leave_w):
    through = enter_w[..., -1]
    pushed = jnp.einsum("khq,kqn,kqhp->khnp", leave_w, write_part, input_part, precision=PRECISE)
    pulled = jnp.einsum("khq,kqn,kqhp->khnp", enter_w, read_part, grad_part, precision=PRECISE)
    return (through, pushed, pulled)


def piece_grads(
    input_part, write_part, read_part, grad_part, lower_mat, enter_w, leave_w, start_state, end_grad
):
    span_len = lower_mat.shape[-1]
    pair_xy = jnp.einsum("kthp,kahp->khta", grad_part, input_part, precision=PRECISE)
    weighted = lower_mat * pair_xy
    cross_dot = jnp.einsum("ktn,kan->kta", read_part, write_part, precision=PRECISE)
    state_dy = jnp.einsum("khnp,kthp->kthn", start_state, grad_part, precision=PRECISE)
    grad_state = jnp.einsum("khnp,kthp->kthn", end_grad, input_part, precision=PRECISE)
    grad_c = jnp.einsum("khta,kan->ktn", weighted, write_part, precision=PRECISE)
    grad_c = grad_c + jnp.einsum("kht,kthn->ktn", enter_w, state_dy, precision=PRECISE)
    grad_b = jnp.einsum("khat,kan->ktn", weighted, read_part, precision=PRECISE)
    grad_b = grad_b + jnp.einsum("kht,kthn->ktn", leave_w, grad_state, precision=PRECISE)
    grad_x = jnp.einsum(
        "khat,kahp->kthp", lower_mat * cross_dot[:, None], grad_part, precision=PRECISE
    )
    end_back = jnp.einsum("khnp,ktn->kthp", end_grad, write_part, precision=PRECISE)
    grad_x = grad_x + jnp.swapaxes(leave_w, 1, 2)[..., None] * end_back
    pair_terms = weighted * cross_dot[:, None]
    strict = jnp.arange(span_len)[None, :] < jnp.arange(span_len)[:, None]
    below_sum = lax.cumsum(pair_terms, axis=2, reverse=True)
    inner_sum = jnp.sum(jnp.where(strict, below_sum, 0.0), axis=-1)
    from_start = enter_w * jnp.einsum("ktn,kthn->kht", read_part, state_dy, precision=PRECISE)
    to_end = leave_w * jnp.einsum("ktn,kthn->kht", write_part, grad_state, precision=PRECISE)
    whole_term = enter_w[..., -1] * jnp.sum(end_grad * start_state, axis=(2, 3))
    later_sum = lax.cumsum(from_start, axis=2, reverse=True)
    earlier_sum = jnp.cumsum(to_end, axis=2) - to_end
    grad_l = inner_sum + later_sum + earlier_sum + whole_term[..., None]
    return (grad_x, grad_b, grad_c, grad_l)


def forward_join(earlier, latter):
    return (earlier[0] * latter[0], latter[0][:, None, None] * earlier[1] + latter[1])


def backward_join(earlier, latter):
    return (latter[0] * earlier[0], latter[1] + latter[0][:, None, None] * earlier[1])


def body(
    queries,
    key_rows,
    value_rows,
    out_grad,
    ssm_input,
    state_write,
    state_read,
    log_decay,
    block_lists,
    rec_lengths,
):
    frames = queries.shape[0]
    span = queries.shape[1]
    head_count = log_decay.shape[0]
    head_size = span // head_count
    blocks_dev = block_lists.shape[0]
    listed_count = block_lists.shape[1]
    block_len = frames // blocks_dev
    win_dev = KWIN // blocks_dev + 1
    win_blocks = win_dev * blocks_dev
    group_size = min(4, head_count)
    device = lax.axis_index("seq")
    score_scale = head_size ** (-0.5)
    query_pos = device * frames + jnp.arange(frames, dtype=jnp.int32)
    query_rec = recording_of(query_pos, rec_lengths)
    key_sets = [(key_rows, value_rows)]
    for distance in range(1, win_dev):
        key_sets.append(passed_along((key_rows, value_rows), "seq", distance))
    ordered = key_sets[::-1]
    win_keys = jnp.concatenate([key_pair[0] for key_pair in ordered], axis=0)
    win_values = jnp.concatenate([key_pair[1] for key_pair in ordered], axis=0)
    win_first = (device - win_dev + 1) * blocks_dev
    listed = block_lists >= 0
    slot_ids = jnp.clip(block_lists - win_first, 0, win_blocks - 1)
    key_pos = (
        block_lists[:, :, None] * block_len + jnp.arange(block_len, dtype=jnp.int32)
    ).reshape(blocks_dev, listed_count * block_len)
    key_rec = recording_of(key_pos, rec_lengths)
    listed_cols = jnp.repeat(listed, block_len, axis=1)
    block_pos = query_pos.reshape(blocks_dev, block_len)
    block_rec = query_rec.reshape(blocks_dev, block_len)
    allowed = (
        listed_cols[:, None, :]
        & (key_rec[:, None, :] == block_rec[:, :, None])
        & (key_pos[:, None, :] <= block_pos[:, :, None])
    )
    mask_b = allowed[:, None]
    gathered_k = win_keys.reshape(win_blocks, block_len, span)[slot_ids].reshape(
        blocks_dev, listed_count * block_len, head_count, head_size
    )
    gathered_v = win_values.reshape(win_blocks, block_len, span)[slot_ids].reshape(
        blocks_dev, listed_count * block_len, head_count, head_size
    )
    query_heads = queries.reshape(blocks_dev, block_len, head_count, head_size)
    grad_heads = out_grad.reshape(blocks_dev, block_len, head_count, head_size)
    grad_q_parts = []
    key_grad_parts = []
    value_grad_parts = []
    for first_head in range(0, head_count, group_size):
        head_cols = slice(first_head, first_head + group_size)
        scores = (
            jnp.einsum(
                "jqhp,jkhp->jhqk",
                query_heads[:, :, head_cols],
                gathered_k[:, :, head_cols],
                preferred_element_type=jnp.float32,
            )
            * score_scale
        )
        exp_score = jnp.where(mask_b, jnp.exp(jnp.where(mask_b, scores, 0.0)), 0.0)
        denominator = jnp.sum(exp_score, axis=-1)
        weights = exp_score / denominator[..., None]
        grad_prob = jnp.einsum(
            "jqhp,jkhp->jhqk",
            grad_heads[:, :, head_cols],
            gathered_v[:, :, head_cols],
            preferred_element_type=jnp.float32,
        )
        row_delta = jnp.sum(weights * grad_prob, axis=-1)
        grad_score = (weights * (grad_prob - row_delta[..., None]) * score_scale).astype(
            jnp.bfloat16
        )
        grad_q_parts.append(
            jnp.einsum(
                "jhqk,jkhp->jqhp",
                grad_score,
                gathered_k[:, :, head_cols],
                preferred_element_type=jnp.float32,
            )
        )
        key_grad_parts.append(
            jnp.einsum(
                "jhqk,jqhp->jkhp",
                grad_score,
                query_heads[:, :, head_cols],
                preferred_element_type=jnp.float32,
            )
        )
        value_grad_parts.append(
            jnp.einsum(
                "jhqk,jqhp->jkhp",
                weights.astype(jnp.bfloat16),
                grad_heads[:, :, head_cols],
                preferred_element_type=jnp.float32,
            )
        )
    grad_queries = jnp.concatenate(grad_q_parts, axis=2).reshape(frames, span).astype(jnp.bfloat16)
    key_grad = jnp.concatenate(key_grad_parts, axis=2).reshape(
        blocks_dev * listed_count, block_len * span
    )
    value_grad = jnp.concatenate(value_grad_parts, axis=2).reshape(
        blocks_dev * listed_count, block_len * span
    )
    owner_hit = (slot_ids.reshape(-1)[:, None] == jnp.arange(win_blocks)[None, :]) & listed.reshape(
        -1
    )[:, None]
    owner_f = owner_hit.astype(jnp.float32)
    win_dk = (
        jnp.einsum("ew,ef->wf", owner_f, key_grad, precision=PRECISE)
        .reshape(win_dev, frames, span)
        .astype(jnp.bfloat16)
    )
    win_dv = (
        jnp.einsum("ew,ef->wf", owner_f, value_grad, precision=PRECISE)
        .reshape(win_dev, frames, span)
        .astype(jnp.bfloat16)
    )
    own_k, own_v = lax.optimization_barrier((win_dk[win_dev - 1], win_dv[win_dev - 1]))
    total_k = own_k.astype(jnp.float32)
    total_v = own_v.astype(jnp.float32)
    for distance in range(1, win_dev):
        back_k, back_v = passed_along(
            (win_dk[win_dev - 1 - distance], win_dv[win_dev - 1 - distance]), "seq", -distance
        )
        total_k = total_k + back_k.astype(jnp.float32)
        total_v = total_v + back_v.astype(jnp.float32)
    grad_keys = total_k.astype(jnp.bfloat16)
    grad_values = total_v.astype(jnp.bfloat16)
    keep_mask = keep_of(query_pos, rec_lengths)
    piece_count = frames // block_len
    input_pieces = ssm_input.astype(jnp.float32).reshape(
        piece_count, block_len, head_count, head_size
    )
    write_pieces = state_write.astype(jnp.float32).reshape(piece_count, block_len, -1)
    read_pieces = state_read.astype(jnp.float32).reshape(piece_count, block_len, -1)
    grad_pieces = out_grad.astype(jnp.float32).reshape(
        piece_count, block_len, head_count, head_size
    )
    decay_pieces = jnp.transpose(log_decay.reshape(head_count, piece_count, block_len), (1, 0, 2))
    keep_pieces = keep_mask.reshape(piece_count, block_len)
    rec_pieces = query_rec.reshape(piece_count, block_len)
    lower_mat, enter_w, leave_w = piece_setup(decay_pieces, keep_pieces, rec_pieces)
    through, pushed, pulled = piece_summary(
        input_pieces, write_pieces, read_pieces, grad_pieces, enter_w, leave_w
    )
    unit_decay = jnp.ones((head_count,), jnp.float32)
    zero_state = jnp.zeros(pushed.shape[1:], jnp.float32)

    def step_forward(running, element):
        return (
            (running[0] * element[0], element[0][:, None, None] * running[1] + element[1]),
            running,
        )

    (dev_decay, dev_state), before = lax.scan(
        step_forward, (unit_decay, zero_state), (through, pushed)
    )

    def step_backward(running, element):
        return (
            (element[0] * running[0], element[1] + element[0][:, None, None] * running[1]),
            running,
        )

    (rev_decay, rev_grad), suffix = lax.scan(
        step_backward, (unit_decay, zero_state), (through, pulled), reverse=True
    )
    state_scan = carried_in(
        (dev_decay, dev_state), "seq", forward_join, (unit_decay, zero_state), False
    )
    grad_scan = carried_in(
        (rev_decay, rev_grad), "seq", backward_join, (unit_decay, zero_state), True
    )
    state_in = state_scan[1]
    grad_in = grad_scan[1]
    start_states = before[0][:, :, None, None] * state_in[None] + before[1]
    end_grads = suffix[0][:, :, None, None] * grad_in[None] + suffix[1]
    grad_x, grad_b, grad_c, grad_l = piece_grads(
        input_pieces,
        write_pieces,
        read_pieces,
        grad_pieces,
        lower_mat,
        enter_w,
        leave_w,
        start_states,
        end_grads,
    )
    grad_input = grad_x.reshape(frames, span).astype(jnp.bfloat16)
    grad_write = grad_b.reshape(frames, -1).astype(jnp.bfloat16)
    grad_read = grad_c.reshape(frames, -1).astype(jnp.bfloat16)
    grad_decay = jnp.transpose(grad_l, (1, 0, 2)).reshape(head_count, frames)
    return (grad_queries, grad_keys, grad_values, grad_input, grad_write, grad_read, grad_decay)


def solution(mesh):
    return jax.shard_map(
        body,
        mesh=mesh,
        in_specs=(
            P(("grp", "seq"), None),
            P(("grp", "seq"), None),
            P(("grp", "seq"), None),
            P(("grp", "seq"), None),
            P(("grp", "seq"), None),
            P(("grp", "seq"), None),
            P(("grp", "seq"), None),
            P(None, ("grp", "seq")),
            P(("grp", "seq"), None),
            P("grp"),
        ),
        out_specs=(
            P(("grp", "seq"), None),
            P(("grp", "seq"), None),
            P(("grp", "seq"), None),
            P(("grp", "seq"), None),
            P(("grp", "seq"), None),
            P(("grp", "seq"), None),
            P(None, ("grp", "seq")),
        ),
        check_vma=False,
    )
```

profile of v0, /device:TPU:3, one launch (start us, length us, event | category | flops | bytes accessed | tf_op | source)
XLA Modules:
  0.0 231.1 jit_solution(10590938283358897472)
XLA Ops:
  16.6 3.2 %collective-permute-start = (bf16[128,768]{1,0:T(8,128)(2,1)S(1)}, bf16[128,768]{1,0:T(8,128)(2,1)S(1)}, u32[]{:S(2)}, u32[]{:S(2)}) collective-permute-start(bf16[128,768]{1,0:T(8,128)(2,1)S(1)} %copy-done.12), channel_id=1, source_target_pairs={{0,4},{1,5},{2,6},{3,7},{4,8},{5,9},{6,10},{7,11},{8,12},{9,13},{1... | collective-permute-start | bytes 589832 | tf_op jit(solution)/shard_map/ppermute | solution.py:15
  19.8 4.0 %collective-permute-start.1 = (bf16[128,768]{1,0:T(8,128)(2,1)S(1)}, bf16[128,768]{1,0:T(8,128)(2,1)S(1)}, u32[]{:S(2)}, u32[]{:S(2)}) collective-permute-start(bf16[128,768]{1,0:T(8,128)(2,1)S(1)} %copy-done.12), channel_id=1, source_target_pairs={{0,3},{1,4},{2,5},{3,6},{4,7},{5,8},{6,9},{7,10},{8,11},{9,12},{10... | collective-permute-start | bytes 589832 | tf_op jit(solution)/shard_map/ppermute | solution.py:15
  23.9 3.2 %collective-permute-start.2 = (bf16[128,768]{1,0:T(8,128)(2,1)S(1)}, bf16[128,768]{1,0:T(8,128)(2,1)S(1)}, u32[]{:S(2)}, u32[]{:S(2)}) collective-permute-start(bf16[128,768]{1,0:T(8,128)(2,1)S(1)} %copy-done.12), channel_id=1, source_target_pairs={{0,2},{1,3},{2,4},{3,5},{4,6},{5,7},{6,8},{7,9},{8,10},{9,11},{10,... | collective-permute-start | bytes 589832 | tf_op jit(solution)/shard_map/ppermute | solution.py:15
  27.0 2.8 %collective-permute-start.3 = (bf16[128,768]{1,0:T(8,128)(2,1)S(1)}, bf16[128,768]{1,0:T(8,128)(2,1)S(1)}, u32[]{:S(2)}, u32[]{:S(2)}) collective-permute-start(bf16[128,768]{1,0:T(8,128)(2,1)S(1)} %copy-done.12), channel_id=1, source_target_pairs={{0,1},{1,2},{2,3},{3,4},{4,5},{5,6},{6,7},{7,8},{8,9},{9,10},{10,1... | collective-permute-start | bytes 589832 | tf_op jit(solution)/shard_map/ppermute | solution.py:15
  29.9 2.5 %collective-permute-start.4 = (bf16[128,768]{1,0:T(8,128)(2,1)S(1)}, bf16[128,768]{1,0:T(8,128)(2,1)S(1)}, u32[]{:S(2)}, u32[]{:S(2)}) collective-permute-start(bf16[128,768]{1,0:T(8,128)(2,1)S(1)} %copy-done.13), channel_id=1, source_target_pairs={{0,4},{1,5},{2,6},{3,7},{4,8},{5,9},{6,10},{7,11},{8,12},{9,13},{1... | collective-permute-start | bytes 589832 | tf_op jit(solution)/shard_map/ppermute | solution.py:15
  34.0 2.9 %select_reduce_fusion = f32[12,128]{0,1:T(8,128)S(1)} fusion(pred[128,128]{1,0:T(8,128)(4,1)S(1)} %iota_compare_fusion, f32[1,12,128,128]{3,2,1,0:T(8,128)S(1)} %get-tuple-element.349), kind=kOutput, calls=%fused_computation.76 | output fusion | flops 25360896 | bytes 808960 | tf_op jit(solution)/shard_map/piece_grads/reduce_window_sum | solution.py:87
  39.6 25.9 %all-gather = f32[16,12,1]{1,2,0:T(1,128)} all-gather(f32[1,12,1]{1,2,0:T(1,128)S(1)} %copy.238), channel_id=2, replica_groups=mesh['grp'=2,'seq'=16] {'seq'}, dimensions={0}, use_global_device_ids=true | all-gather | bytes 816 | tf_op jit(solution)/shard_map/all_gather | solution.py:22
  65.5 1.9 collective-permute-start.5
  69.4 2.9 %collective-permute-start.7 = (bf16[128,768]{1,0:T(8,128)(2,1)S(1)}, bf16[128,768]{1,0:T(8,128)(2,1)S(1)}, u32[]{:S(2)}, u32[]{:S(2)}) collective-permute-start(bf16[128,768]{1,0:T(8,128)(2,1)S(1)} %copy-done.13), channel_id=1, source_target_pairs={{0,1},{1,2},{2,3},{3,4},{4,5},{5,6},{6,7},{7,8},{8,9},{9,10},{10,1... | collective-permute-start | bytes 589832 | tf_op jit(solution)/shard_map/ppermute | solution.py:15
  74.8 3.2 %collective-permute-done.5 = bf16[128,768]{1,0:T(8,128)(2,1)} collective-permute-done((bf16[128,768]{1,0:T(8,128)(2,1)S(1)}, bf16[128,768]{1,0:T(8,128)(2,1)}, u32[]{:S(2)}, u32[]{:S(2)}) %collective-permute-start.5) | collective-permute-done | bytes 196640 | tf_op jit(solution)/shard_map/ppermute | solution.py:15
  78.9 5.7 %collective-permute-done.6 = bf16[128,768]{1,0:T(8,128)(2,1)S(1)} collective-permute-done((bf16[128,768]{1,0:T(8,128)(2,1)S(1)}, bf16[128,768]{1,0:T(8,128)(2,1)S(1)}, u32[]{:S(2)}, u32[]{:S(2)}) %collective-permute-start.6) | collective-permute-done | bytes 196640 | tf_op jit(solution)/shard_map/ppermute | solution.py:15
  84.6 6.3 %collective-permute-done.7 = bf16[128,768]{1,0:T(8,128)(2,1)S(1)} collective-permute-done((bf16[128,768]{1,0:T(8,128)(2,1)S(1)}, bf16[128,768]{1,0:T(8,128)(2,1)S(1)}, u32[]{:S(2)}, u32[]{:S(2)}) %collective-permute-start.7) | collective-permute-done | bytes 196640 | tf_op jit(solution)/shard_map/ppermute | solution.py:15
  94.7 2.2 convolution_bitcast_fusion.6
  97.3 2.8 %fusion.68 = f32[4,128,512]{1,2,0:T(8,128)} fusion(pred[128,512]{0,1:T(8,128)(4,1)} %compare_and_fusion, bf16[1,512,12,64]{1,3,2,0:T(8,128)(2,1)} %reshape.828, bf16[1,128,12,64]{1,3,2,0:T(8,128)(2,1)} %bitcast.399), kind=kOutput, calls=%fused_computation.101 | convolution fusion | flops 34604032 | bytes 1441792 | tf_op jit(solution)/shard_map/div | solution.py:178
  100.1 2.9 %convolution_bitcast_fusion.7 = f32[1,512,4,64]{1,3,2,0:T(8,128)} fusion(f32[4,128,512]{1,2,0:T(8,128)} %fusion.68, f32[4,128,512]{1,2,0:T(8,128)S(1)} %convolution_bitcast_fusion.1, bf16[1,128,12,64]{1,3,2,0:T(8,128)(2,1)} %bitcast.400), kind=kOutput, calls=%fused_computation.50 | convolution fusion | flops 34866176 | bytes 4784128 | tf_op jit(solution)/shard_map/jhqk,jqhp->jkhp/dot_general | solution.py:198
  105.1 2.1 convolution_bitcast_fusion.8
  108.9 3.7 %copy.232 = f32[1,512,12,64]{3,2,1,0:T(8,128)} copy(f32[1,512,12,64]{1,3,2,0:T(8,128)S(1)} %pad_maximum_fusion) | data formatting | bytes 3145728 | tf_op jit(solution)/shard_map/concatenate | solution.py:214
  112.6 3.6 %reshape.846 = f32[4,98304]{1,0:T(4,128)S(1)} reshape(f32[1,512,12,64]{3,2,1,0:T(8,128)} %copy.232) | data formatting | bytes 3145728 | tf_op jit(solution)/shard_map/reshape | solution.py:214
  116.3 2.0 convolution_convert_fusion.1
  127.7 2.1 collective-permute-start.8
  131.0 3.7 %copy.236 = f32[1,512,12,64]{3,2,1,0:T(8,128)} copy(f32[1,512,12,64]{1,3,2,0:T(8,128)S(1)} %pad_maximum_fusion.1) | data formatting | bytes 3145728 | tf_op jit(solution)/shard_map/concatenate | solution.py:217
  134.7 3.7 %reshape.847 = f32[4,98304]{1,0:T(4,128)S(1)} reshape(f32[1,512,12,64]{3,2,1,0:T(8,128)} %copy.236) | data formatting | bytes 3145728 | tf_op jit(solution)/shard_map/reshape | solution.py:217
  138.5 2.7 %fusion.37 = bf16[1,128,4,64]{1,3,2,0:T(8,128)(2,1)S(1)} fusion(f32[4,128,512]{1,2,0:T(8,128)} %copy-done.3, f32[4,128,512]{1,2,0:T(8,128)} %copy-done.2, bf16[1,512,12,64]{1,3,2,0:T(8,128)(2,1)S(1)} %copy-done.8), kind=kOutput, calls=%fused_computation.69 | convolution fusion | flops 34898944 | bytes 4521984 | tf_op jit(solution)/shard_map/jhqk,jkhp->jqhp/dot_general | solution.py:190
  141.2 2.7 %fusion.36 = bf16[1,128,4,64]{1,3,2,0:T(8,128)(2,1)S(1)} fusion(f32[4,128,512]{1,2,0:T(8,128)} %fusion.68, f32[4,128,512]{1,2,0:T(8,128)} %copy-done.5, bf16[1,512,12,64]{1,3,2,0:T(8,128)(2,1)S(1)} %copy-done.8), kind=kOutput, calls=%fused_computation.68 | convolution fusion | flops 34898944 | bytes 4521984 | tf_op jit(solution)/shard_map/jhqk,jkhp->jqhp/dot_general | solution.py:190
  143.9 2.7 %convolution_convert_fusion = bf16[5,128,768]{2,0,1:T(8,128)(2,1)S(1)} fusion(f32[128,768,4]{1,2,0:T(4,128)S(1)} %bitcast.375, s32[4]{0:T(128)} %get-tuple-element.359, pred[4]{0:T(512)(128)(4,1)} %copy-done.28), kind=kOutput, calls=%fused_computation.11 | convolution fusion | flops 24084520 | bytes 2555924 | tf_op jit(solution)/shard_map/ew,ef->wf/dot_general | solution.py:230
  148.1 2.7 %fusion.35 = bf16[1,128,4,64]{1,3,2,0:T(8,128)(2,1)S(1)} fusion(f32[4,128,512]{1,2,0:T(8,128)} %copy-done.1, f32[4,128,512]{1,2,0:T(8,128)} %copy-done, bf16[1,512,12,64]{1,3,2,0:T(8,128)(2,1)} %reshape.828), kind=kOutput, calls=%fused_computation.67 | convolution fusion | flops 34898944 | bytes 4521984 | tf_op jit(solution)/shard_map/jhqk,jkhp->jqhp/dot_general | solution.py:190
  155.1 1.9 collective-permute-start.13
  159.0 2.1 add_convert_fusion.1
  161.0 7.1 %collective-permute-done.15 = bf16[128,768]{1,0:T(8,128)(2,1)S(1)} collective-permute-done((bf16[128,768]{1,0:T(8,128)(2,1)S(1)}, bf16[128,768]{1,0:T(8,128)(2,1)S(1)}, u32[]{:S(2)}, u32[]{:S(2)}) %collective-permute-start.15) | collective-permute-done | bytes 196640 | tf_op jit(solution)/shard_map/ppermute | solution.py:15
  170.0 9.3 %collective-permute-done.13 = bf16[128,768]{1,0:T(8,128)(2,1)S(1)} collective-permute-done((bf16[128,768]{1,0:T(8,128)(2,1)S(1)}, bf16[128,768]{1,0:T(8,128)(2,1)S(1)}, u32[]{:S(2)}, u32[]{:S(2)}) %collective-permute-start.13) | collective-permute-done | bytes 196640 | tf_op jit(solution)/shard_map/ppermute | solution.py:15
  182.0 26.4 %while.16 = (s32[]{:T(128)}, f32[12,128,64]{2,1,0:T(8,128)S(1)}, s32[]{:T(128)}, f32[16,12,128,64]{2,3,1,0:T(8,128)}, f32[16,12]{1,0:T(8,128)}, /*index=5*/s32[]{:T(128)}, s32[]{:T(128)}, s32[]{:T(128)}, s32[]{:T(128)}) while((s32[]{:T(128)}, f32[12,128,64]{2,1,0:T(8,128)S(1)}, s32[]{:T(128)}, f32[16,12,128,64]{2,3,1,0:T(8,128)}, ...), condition=%wide.region_12.13_spmd, body=%wide.region_11.12_spmd.sunk | while | flops 196614 | bytes 2752811 | solution.py:31
  208.5 6.9 %while.17 = (s32[]{:T(128)}, f32[12,128,64]{2,1,0:T(8,128)S(1)}, s32[]{:T(128)}, f32[16,12]{1,0:T(8,128)}, f32[16,12,128,64]{2,3,1,0:T(8,128)}, /*index=5*/s32[]{:T(128)}, s32[]{:T(128)}, s32[]{:T(128)}) while((s32[]{:T(128)}, f32[12,128,64]{2,1,0:T(8,128)S(1)}, s32[]{:T(128)}, f32[16,12]{1,0:T(8,128)}, f32[16,12,128,64]{2,3,1,0:T(8,128)}, ...), condition=%wide.region_15.16_spmd, body=%wide.region_14.15_spmd.sunk | while | flops 196613 | bytes 2752791 | solution.py:31
  (248 shorter events, 90.4 us)
Async XLA Ops:
  7.2 26.1 %copy-start.9 = (bf16[128,128]{1,0:T(8,128)(2,1)S(1)}, bf16[128,128]{1,0:T(8,128)(2,1)}, u32[]{:S(2)}) copy-start(bf16[128,128]{1,0:T(8,128)(2,1)} %param.20) | copy-start | bytes 98308
  7.2 8.1 %copy-start.10 = (bf16[128,768]{1,0:T(8,128)(2,1)S(1)}, bf16[128,768]{1,0:T(8,128)(2,1)}, u32[]{:S(2)}) copy-start(bf16[128,768]{1,0:T(8,128)(2,1)} %param.18) | copy-start | bytes 589828
  7.2 8.3 %copy-start.7 = (bf16[128,128]{1,0:T(8,128)(2,1)S(1)}, bf16[128,128]{1,0:T(8,128)(2,1)}, u32[]{:S(2)}) copy-start(bf16[128,128]{1,0:T(8,128)(2,1)} %param.19) | copy-start | bytes 98308
  7.2 9.4 %copy-start.12 = (bf16[128,768]{1,0:T(8,128)(2,1)S(1)}, bf16[128,768]{1,0:T(8,128)(2,1)}, u32[]{:S(2)}) copy-start(bf16[128,768]{1,0:T(8,128)(2,1)} %param.15) | copy-start | bytes 589828
  7.2 22.7 %copy-start.13 = (bf16[128,768]{1,0:T(8,128)(2,1)S(1)}, bf16[128,768]{1,0:T(8,128)(2,1)}, u32[]{:S(2)}) copy-start(bf16[128,768]{1,0:T(8,128)(2,1)} %param.16) | copy-start | bytes 589828
  7.2 25.2 %copy-start.33 = (s32[1,4]{1,0:T(1,128)S(1)}, s32[1,4]{1,0:T(1,128)}, u32[]{:S(2)}) copy-start(s32[1,4]{1,0:T(1,128)} %param.22) | copy-start | bytes 52
  7.2 174.7 %all-gather.4.cloned.1.call-start = ((), (), s32[]{:S(2)}) async-start(), calls=%async_computation | async-start | bytes 6684672 | tf_op jit(solution)/shard_map/all_gather | solution.py:22
  11.3 21.6 %copy-start.26 = (f32[12]{0:T(128)}, f32[12]{0:T(128)S(1)}, u32[]{:S(2)}) copy-start(f32[12]{0:T(128)S(1)} %slice_reduce_fusion) | copy-start | bytes 148
  12.0 21.0 %copy-start.23 = (f32[128]{0:T(128)}, f32[128]{0:T(128)S(1)}, u32[]{:S(2)}) copy-start(f32[128]{0:T(128)S(1)} %compare_select_fusion.1) | copy-start | bytes 1540
  13.3 19.8 %copy-start.30 = (f32[128]{0:T(128)}, f32[128]{0:T(128)S(1)}, u32[]{:S(2)}) copy-start(f32[128]{0:T(128)S(1)} %compare_convert_fusion) | copy-start | bytes 1540
  13.4 20.0 %copy-start.14 = (f32[128,12]{0,1:T(8,128)}, f32[128,12]{0,1:T(8,128)S(1)}, u32[]{:S(2)}) copy-start(f32[128,12]{0,1:T(8,128)S(1)} %get-tuple-element.354) | copy-start | bytes 18436
  15.2 193.2 %all-gather.6.cloned.1.call-start = ((), (), s32[]{:S(2)}) async-start(), calls=%async_computation.1 | async-start | bytes 6684672 | tf_op jit(solution)/shard_map/all_gather | solution.py:22
  16.6 48.9 %collective-permute-start = (bf16[128,768]{1,0:T(8,128)(2,1)S(1)}, bf16[128,768]{1,0:T(8,128)(2,1)S(1)}, u32[]{:S(2)}, u32[]{:S(2)}) collective-permute-start(bf16[128,768]{1,0:T(8,128)(2,1)S(1)} %copy-done.12), channel_id=1, source_target_pairs={{0,4},{1,5},{2,6},{3,7},{4,8},{5,9},{6,10},{7,11},{8,12},{9,13},{1... | collective-permute-start | bytes 589832 | tf_op jit(solution)/shard_map/ppermute | solution.py:15
  19.8 47.6 %collective-permute-start.1 = (bf16[128,768]{1,0:T(8,128)(2,1)S(1)}, bf16[128,768]{1,0:T(8,128)(2,1)S(1)}, u32[]{:S(2)}, u32[]{:S(2)}) collective-permute-start(bf16[128,768]{1,0:T(8,128)(2,1)S(1)} %copy-done.12), channel_id=1, source_target_pairs={{0,3},{1,4},{2,5},{3,6},{4,7},{5,8},{6,9},{7,10},{8,11},{9,12},{10... | collective-permute-start | bytes 589832 | tf_op jit(solution)/shard_map/ppermute | solution.py:15
  23.9 45.5 %collective-permute-start.2 = (bf16[128,768]{1,0:T(8,128)(2,1)S(1)}, bf16[128,768]{1,0:T(8,128)(2,1)S(1)}, u32[]{:S(2)}, u32[]{:S(2)}) collective-permute-start(bf16[128,768]{1,0:T(8,128)(2,1)S(1)} %copy-done.12), channel_id=1, source_target_pairs={{0,2},{1,3},{2,4},{3,5},{4,6},{5,7},{6,8},{7,9},{8,10},{9,11},{10,... | collective-permute-start | bytes 589832 | tf_op jit(solution)/shard_map/ppermute | solution.py:15
  27.0 45.2 %collective-permute-start.3 = (bf16[128,768]{1,0:T(8,128)(2,1)S(1)}, bf16[128,768]{1,0:T(8,128)(2,1)S(1)}, u32[]{:S(2)}, u32[]{:S(2)}) collective-permute-start(bf16[128,768]{1,0:T(8,128)(2,1)S(1)} %copy-done.12), channel_id=1, source_target_pairs={{0,1},{1,2},{2,3},{3,4},{4,5},{5,6},{6,7},{7,8},{8,9},{9,10},{10,1... | collective-permute-start | bytes 589832 | tf_op jit(solution)/shard_map/ppermute | solution.py:15
  29.9 44.9 %collective-permute-start.4 = (bf16[128,768]{1,0:T(8,128)(2,1)S(1)}, bf16[128,768]{1,0:T(8,128)(2,1)S(1)}, u32[]{:S(2)}, u32[]{:S(2)}) collective-permute-start(bf16[128,768]{1,0:T(8,128)(2,1)S(1)} %copy-done.13), channel_id=1, source_target_pairs={{0,4},{1,5},{2,6},{3,7},{4,8},{5,9},{6,10},{7,11},{8,12},{9,13},{1... | collective-permute-start | bytes 589832 | tf_op jit(solution)/shard_map/ppermute | solution.py:15
  33.9 38.4 %copy-start.28 = (pred[4]{0:T(512)(128)(4,1)}, pred[4]{0:T(512)(128)(4,1)S(1)}, u32[]{:S(2)}) copy-start(pred[4]{0:T(512)(128)(4,1)S(1)} %compare_bitcast_fusion) | copy-start | bytes 16
  65.5 12.5 %collective-permute-start.5 = (bf16[128,768]{1,0:T(8,128)(2,1)S(1)}, bf16[128,768]{1,0:T(8,128)(2,1)}, u32[]{:S(2)}, u32[]{:S(2)}) collective-permute-start(bf16[128,768]{1,0:T(8,128)(2,1)S(1)} %copy-done.13), channel_id=1, source_target_pairs={{0,3},{1,4},{2,5},{3,6},{4,7},{5,8},{6,9},{7,10},{8,11},{9,12},{10... | collective-permute-start | bytes 589832 | tf_op jit(solution)/shard_map/ppermute | solution.py:15
  67.4 17.2 %collective-permute-start.6 = (bf16[128,768]{1,0:T(8,128)(2,1)S(1)}, bf16[128,768]{1,0:T(8,128)(2,1)S(1)}, u32[]{:S(2)}, u32[]{:S(2)}) collective-permute-start(bf16[128,768]{1,0:T(8,128)(2,1)S(1)} %copy-done.13), channel_id=1, source_target_pairs={{0,2},{1,3},{2,4},{3,5},{4,6},{5,7},{6,8},{7,9},{8,10},{9,11},{10,... | collective-permute-start | bytes 589832 | tf_op jit(solution)/shard_map/ppermute | solution.py:15
  69.4 21.5 %collective-permute-start.7 = (bf16[128,768]{1,0:T(8,128)(2,1)S(1)}, bf16[128,768]{1,0:T(8,128)(2,1)S(1)}, u32[]{:S(2)}, u32[]{:S(2)}) collective-permute-start(bf16[128,768]{1,0:T(8,128)(2,1)S(1)} %copy-done.13), channel_id=1, source_target_pairs={{0,1},{1,2},{2,3},{3,4},{4,5},{5,6},{6,7},{7,8},{8,9},{9,10},{10,1... | collective-permute-start | bytes 589832 | tf_op jit(solution)/shard_map/ppermute | solution.py:15
  105.1 25.3 %copy-start.1 = (f32[4,128,512]{1,2,0:T(8,128)}, f32[4,128,512]{1,2,0:T(8,128)S(1)}, u32[]{:S(2)}) copy-start(f32[4,128,512]{1,2,0:T(8,128)S(1)} %fusion.76) | copy-start | bytes 3145732
  119.8 10.1 %copy-start.4 = (f32[4,128,512]{1,2,0:T(8,128)S(1)}, f32[4,128,512]{1,2,0:T(8,128)}, u32[]{:S(2)}) copy-start(f32[4,128,512]{1,2,0:T(8,128)} %copy-done.3) | copy-start | bytes 3145732
  120.5 32.7 %collective-permute-start.11 = (bf16[128,768]{1,0:T(8,128)(2,1)}, bf16[128,768]{1,0:T(8,128)(2,1)}, u32[]{:S(2)}, u32[]{:S(2)}) collective-permute-start(bf16[128,768]{1,0:T(8,128)(2,1)} %bitcast.360), channel_id=1, source_target_pairs={{4,0},{5,1},{6,2},{7,3},{8,4},{9,5},{10,6},{11,7},{12,8},{13,9},{1... | collective-permute-start | bytes 589832 | tf_op jit(solution)/shard_map/ppermute | solution.py:15
  121.8 8.4 %copy-start.6 = (f32[4,128,512]{1,2,0:T(8,128)S(1)}, f32[4,128,512]{1,2,0:T(8,128)}, u32[]{:S(2)}) copy-start(f32[4,128,512]{1,2,0:T(8,128)} %fusion.68) | copy-start | bytes 3145732
  122.5 32.6 %collective-permute-start.10 = (bf16[128,768]{1,0:T(8,128)(2,1)}, bf16[128,768]{1,0:T(8,128)(2,1)}, u32[]{:S(2)}, u32[]{:S(2)}) collective-permute-start(bf16[128,768]{1,0:T(8,128)(2,1)} %bitcast.361), channel_id=1, source_target_pairs={{3,0},{4,1},{5,2},{6,3},{7,4},{8,5},{9,6},{10,7},{11,8},{12,9},{13... | collective-permute-start | bytes 589832 | tf_op jit(solution)/shard_map/ppermute | solution.py:15
  125.1 31.9 %collective-permute-start.9 = (bf16[128,768]{1,0:T(8,128)(2,1)}, bf16[128,768]{1,0:T(8,128)(2,1)}, u32[]{:S(2)}, u32[]{:S(2)}) collective-permute-start(bf16[128,768]{1,0:T(8,128)(2,1)} %bitcast.362), channel_id=1, source_target_pairs={{2,0},{3,1},{4,2},{5,3},{6,4},{7,5},{8,6},{9,7},{10,8},{11,9},{12,... | collective-permute-start | bytes 589832 | tf_op jit(solution)/shard_map/ppermute | solution.py:15
  127.7 31.3 %collective-permute-start.8 = (bf16[128,768]{1,0:T(8,128)(2,1)}, bf16[128,768]{1,0:T(8,128)(2,1)}, u32[]{:S(2)}, u32[]{:S(2)}) collective-permute-start(bf16[128,768]{1,0:T(8,128)(2,1)} %bitcast.363), channel_id=1, source_target_pairs={{1,0},{2,1},{3,2},{4,3},{5,4},{6,5},{7,6},{8,7},{9,8},{10,9},{11,1... | collective-permute-start | bytes 589832 | tf_op jit(solution)/shard_map/ppermute | solution.py:15
  151.8 16.4 %collective-permute-start.15 = (bf16[128,768]{1,0:T(8,128)(2,1)S(1)}, bf16[128,768]{1,0:T(8,128)(2,1)S(1)}, u32[]{:S(2)}, u32[]{:S(2)}) collective-permute-start(bf16[128,768]{1,0:T(8,128)(2,1)S(1)} %bitcast.405), channel_id=1, source_target_pairs={{4,0},{5,1},{6,2},{7,3},{8,4},{9,5},{10,6},{11,7},{12,8},{13,9},{1... | collective-permute-start | bytes 589832 | tf_op jit(solution)/shard_map/ppermute | solution.py:15
  153.2 16.8 %collective-permute-start.14 = (bf16[128,768]{1,0:T(8,128)(2,1)S(1)}, bf16[128,768]{1,0:T(8,128)(2,1)S(1)}, u32[]{:S(2)}, u32[]{:S(2)}) collective-permute-start(bf16[128,768]{1,0:T(8,128)(2,1)S(1)} %bitcast.407), channel_id=1, source_target_pairs={{3,0},{4,1},{5,2},{6,3},{7,4},{8,5},{9,6},{10,7},{11,8},{12,9},{13... | collective-permute-start | bytes 589832 | tf_op jit(solution)/shard_map/ppermute | solution.py:15
  155.1 24.2 %collective-permute-start.13 = (bf16[128,768]{1,0:T(8,128)(2,1)S(1)}, bf16[128,768]{1,0:T(8,128)(2,1)S(1)}, u32[]{:S(2)}, u32[]{:S(2)}) collective-permute-start(bf16[128,768]{1,0:T(8,128)(2,1)S(1)} %bitcast.406), channel_id=1, source_target_pairs={{2,0},{3,1},{4,2},{5,3},{6,4},{7,5},{8,6},{9,7},{10,8},{11,9},{12,... | collective-permute-start | bytes 589832 | tf_op jit(solution)/shard_map/ppermute | solution.py:15
  157.0 24.1 %collective-permute-start.12 = (bf16[128,768]{1,0:T(8,128)(2,1)S(1)}, bf16[128,768]{1,0:T(8,128)(2,1)S(1)}, u32[]{:S(2)}, u32[]{:S(2)}) collective-permute-start(bf16[128,768]{1,0:T(8,128)(2,1)S(1)} %bitcast.404), channel_id=1, source_target_pairs={{1,0},{2,1},{3,2},{4,3},{5,4},{6,5},{7,6},{8,7},{9,8},{10,9},{11,1... | collective-permute-start | bytes 589832 | tf_op jit(solution)/shard_map/ppermute | solution.py:15
  (20 other events, 63.0 us)
Sparse Core Ops, SparseCore 0:
  15.4 78.5 all-gather.3
  96.3 72.3 all-gather.5
where the time goes:
time: 235 us; the launch traced here: 231 us
  local copies, waits for them, and re-layouts  61.9 us (26%)
  starting transfers between devices  36.8 us (16%)
  matrix products  36.2 us (15%)
  waiting for transfers between devices  35.4 us (15%)
  blocking collectives  25.9 us (11%)
  other arithmetic  18.9 us (8%)
  between operations  15.1 us (6%)
    ppermute x16, starting transfers between devices, passed_along(): return lax.ppermute(block, axis, route)  36.7 us
    ppermute x16, waiting for transfers between devices, passed_along(): return lax.ppermute(block, axis, route)  35.3 us
    all_gather x1, blocking collectives, carried_in(): gathered = jax.tree.map(lambda a: lax.all_gather(a, axis), part)  25.9 us
    dynamic_slice x30, local copies, waits for them, and re-layouts, one(): lax.dynamic_index_in_dim(a, source, 0, False)  19.4 us
    unnamed x93, local copies, waits for them, and re-layouts  8.51 us
    mul x12, local copies, waits for them, and re-layouts, backward_join(): latter[0][:, None, None] * earlier[1]  8.22 us
    dot_general x3, matrix products, body(): jnp.einsum('jhqk,jkhp->jqhp', grad_score, gathered_k[:, :, head_cols], pr...  8.11 us
    dot_general x3, matrix products, body(): jnp.einsum('jhqk,jqhp->jkhp', grad_score, query_heads[:, :, head_cols], p...  7.19 us
  transfers between devices with their start and end apart: 18, of which 7 were waited for; matrix products, arithmetic and copies ran while one was open for 41% of the time, Pallas kernels for 0%

commit v1 on v0

v1 whole, which is shorter than its diff:
```python
import functools

import jax
import jax.numpy as jnp
from jax import lax
from jax.experimental import pallas as pl
from jax.experimental.pallas import tpu as pltpu
from jax.sharding import PartitionSpec as P

KWIN = 4
F32 = jnp.float32
BF16 = jnp.bfloat16
HIGH = lax.Precision.HIGHEST


def dot(a, b, dims, precision=None):
    return lax.dot_general(a, b, (dims, ((), ())), precision=precision, preferred_element_type=F32)


NN = ((1,), (0,))
NT = ((1,), (1,))
TN = ((0,), (0,))


def mix_kernel(
    count,
    heads,
    q_ref,
    k_ref,
    v_ref,
    do_ref,
    x_ref,
    b_ref,
    c_ref,
    bias_ref,
    same_ref,
    cum_ref,
    cum_t_ref,
    gq_ref,
    gk_ref,
    gv_ref,
    gx_ref,
    gb_ref,
    gc_ref,
    gl_ref,
    kw,
    vw,
    pk,
    pv,
    rk,
    rv,
    wsum,
    send_sem,
    recv_sem,
    bsend_sem,
    brecv_sem,
):
    me = lax.axis_index("seq")
    rows, width = q_ref.shape
    size = width // heads
    scale = size ** (-0.5)
    own = KWIN * rows

    def place(dist):
        return pl.ds((KWIN - dist) * rows, rows)

    def forward(dist):
        return [
            pltpu.make_async_remote_copy(
                src_ref=src,
                dst_ref=dst.at[place(dist), :],
                send_sem=send_sem.at[dist - 1, i],
                recv_sem=recv_sem.at[dist - 1, i],
                device_id={"seq": me + dist},
                device_id_type=pl.DeviceIdType.MESH,
            )
            for i, (src, dst) in enumerate(((k_ref, kw), (v_ref, vw)))
        ]

    def backward(dist):
        return [
            pltpu.make_async_remote_copy(
                src_ref=src.at[place(dist), :],
                dst_ref=dst.at[dist - 1],
                send_sem=bsend_sem.at[dist - 1, i],
                recv_sem=brecv_sem.at[dist - 1, i],
                device_id={"seq": me - dist},
                device_id_type=pl.DeviceIdType.MESH,
            )
            for i, (src, dst) in enumerate(((pk, rk), (pv, rv)))
        ]

    barrier = pltpu.get_barrier_semaphore()
    for dist in range(1, KWIN + 1):

        @pl.when(me + dist < count)
        def _():
            pl.semaphore_signal(
                barrier, inc=1, device_id={"seq": me + dist}, device_id_type=pl.DeviceIdType.MESH
            )

        @pl.when(me - dist >= 0)
        def _():
            pl.semaphore_signal(
                barrier, inc=1, device_id={"seq": me - dist}, device_id_type=pl.DeviceIdType.MESH
            )

    peers = 0
    for dist in range(1, KWIN + 1):
        peers += (me + dist < count).astype(jnp.int32) + (me - dist >= 0).astype(jnp.int32)
    pl.semaphore_wait(barrier, peers)

    for dist in range(KWIN, 0, -1):

        @pl.when(me + dist < count)
        def _():
            for copy in forward(dist):
                copy.start()

    zero = jnp.zeros((rows, width), BF16)
    for dist in range(1, KWIN + 1):

        @pl.when(me - dist < 0)
        def _():
            kw[place(dist), :] = zero
            vw[place(dist), :] = zero

        @pl.when(me + dist >= count)
        def _():
            rk[dist - 1] = zero
            rv[dist - 1] = zero

    kw[pl.ds(own, rows), :] = k_ref[...]
    vw[pl.ds(own, rows), :] = v_ref[...]

    cross = dot(c_ref[...], b_ref[...], NT)
    row_id = lax.broadcasted_iota(jnp.int32, (rows, rows), 0)
    col_id = lax.broadcasted_iota(jnp.int32, (rows, rows), 1)
    upper = (col_id >= row_id).astype(BF16)
    strict = col_id < row_id
    lane = lax.broadcasted_iota(jnp.int32, (rows, gl_ref.shape[1]), 1)
    wsum[...] = jnp.zeros_like(wsum)
    gl = jnp.zeros(gl_ref.shape, F32)
    for first in range(0, heads, 2):
        cols = slice(first * size, (first + 2) * size)
        do2 = do_ref[:, cols]
        x2 = x_ref[:, cols]
        parts = []
        for i in range(2):
            h = first + i
            half = slice(i * size, (i + 1) * size)
            decay = jnp.exp(cum_t_ref[:, h : h + 1] - cum_ref[h : h + 1, :] + same_ref[...])
            pair = dot(do2[:, half], x2[:, half], NT)
            weighted = decay * pair
            wsum[...] += weighted
            mixed = decay * cross
            parts.append(dot(mixed.astype(BF16), do2[:, half], TN))
            terms = (weighted * cross).astype(BF16)
            below = dot(upper, terms, NN)
            inner = jnp.sum(jnp.where(strict, below, 0.0), axis=1, keepdims=True)
            gl = jnp.where(lane == h, inner, gl)
        gx_ref[:, cols] = jnp.concatenate(parts, axis=1)
    gl_ref[...] = gl
    weighted = wsum[...].astype(BF16)
    gc_ref[...] = dot(weighted, b_ref[...], NN)
    gb_ref[...] = dot(weighted, c_ref[...], TN)

    for dist in range(1, KWIN + 1):

        @pl.when(me - dist >= 0)
        def _():
            for copy in forward(dist):
                copy.wait_recv()

    def pair_of_heads(step, carry):
        cols = pl.ds(pl.multiple_of(step * 2 * size, 2 * size), 2 * size)
        q2, do2 = q_ref[:, cols], do_ref[:, cols]
        k2, v2 = kw[:, cols], vw[:, cols]
        gq, gk, gv = [], [], []
        for i in range(2):
            half = slice(i * size, (i + 1) * size)
            qh, kh, vh, dh = q2[:, half], k2[:, half], v2[:, half], do2[:, half]
            e = jnp.exp(dot(qh, kh, NT) * scale + bias_ref[...])
            prob = e * (1.0 / jnp.sum(e, axis=1, keepdims=True))
            dprob = dot(dh, vh, NT)
            delta = jnp.sum(prob * dprob, axis=1, keepdims=True)
            ds = (prob * (dprob - delta) * scale).astype(BF16)
            gq.append(dot(ds, kh, NN))
            gk.append(dot(ds, qh, TN))
            gv.append(dot(prob.astype(BF16), dh, TN))
        gq_ref[:, cols] = jnp.concatenate(gq, axis=1).astype(BF16)
        pk[:, cols] = jnp.concatenate(gk, axis=1).astype(BF16)
        pv[:, cols] = jnp.concatenate(gv, axis=1).astype(BF16)
        return carry

    lax.fori_loop(0, heads // 2, pair_of_heads, 0)

    for dist in range(KWIN, 0, -1):

        @pl.when(me - dist >= 0)
        def _():
            for copy in backward(dist):
                copy.start()

    for dist in range(1, KWIN + 1):

        @pl.when(me + dist < count)
        def _():
            for copy in forward(dist):
                copy.wait_send()
            for copy in backward(dist):
                copy.wait_recv()

    total_k = pk[pl.ds(own, rows), :].astype(F32)
    total_v = pv[pl.ds(own, rows), :].astype(F32)
    for dist in range(1, KWIN + 1):
        total_k = total_k + rk[dist - 1].astype(F32)
        total_v = total_v + rv[dist - 1].astype(F32)
    gk_ref[...] = total_k.astype(BF16)
    gv_ref[...] = total_v.astype(BF16)

    for dist in range(1, KWIN + 1):

        @pl.when(me - dist >= 0)
        def _():
            for copy in backward(dist):
                copy.wait_send()


def join_kernel(
    heads,
    state_ref,
    grad_ref,
    xl_ref,
    de_ref,
    leave_ref,
    b_ref,
    c_ref,
    through_ref,
    gxi_ref,
    gbi_ref,
    gci_ref,
    gli_ref,
    gx_ref,
    gb_ref,
    gc_ref,
    gl_ref,
):
    rows, width = gx_ref.shape
    size = width // heads
    lanes = gl_ref.shape[1]
    state, grad = state_ref[...], grad_ref[...]
    state_b, grad_b = state.astype(BF16), grad.astype(BF16)
    xl, de = xl_ref[...], de_ref[...]
    gc_ref[...] = (gci_ref[...] + dot(de, state_b, NN)).astype(BF16)
    gb_ref[...] = (gbi_ref[...] + dot(xl, grad_b, NN)).astype(BF16)
    back = dot(b_ref[...], grad_b, NT)
    ahead = dot(c_ref[...], state_b, NT)
    gx_ref[...] = (gxi_ref[...] + leave_ref[...].astype(F32) * back).astype(BF16)
    owner = lax.broadcasted_iota(jnp.int32, (width, lanes), 0) // size
    pick = (owner == lax.broadcasted_iota(jnp.int32, (width, lanes), 1)).astype(F32)
    from_start = dot(de.astype(F32) * ahead, pick, NN, HIGH)
    to_end = dot(xl.astype(F32) * back, pick, NN, HIGH)
    row_id = lax.broadcasted_iota(jnp.int32, (rows, rows), 0)
    col_id = lax.broadcasted_iota(jnp.int32, (rows, rows), 1)
    later = dot((col_id >= row_id).astype(F32), from_start, NN, HIGH)
    earlier = dot((col_id < row_id).astype(F32), to_end, NN, HIGH)
    each = dot(jnp.ones((8, state.shape[1]), F32), grad * state, NT, HIGH)
    whole = dot(each, pick, NN, HIGH)[:1] * through_ref[...]
    gl_ref[...] = gli_ref[...] + later + earlier + whole


def body(
    queries,
    key_rows,
    value_rows,
    out_grad,
    ssm_input,
    state_write,
    state_read,
    log_decay,
    block_lists,
    rec_lengths,
):
    rows, width = queries.shape
    heads = log_decay.shape[0]
    size = width // heads
    states = state_write.shape[1]
    lanes = 128
    count = lax.axis_size("seq")
    me = lax.axis_index("seq")
    assert block_lists.shape[0] == 1

    ends = jnp.sum(
        jnp.where(
            jnp.arange(rec_lengths.shape[0])[:, None] >= jnp.arange(rec_lengths.shape[0])[None, :],
            rec_lengths[None, :],
            0,
        ),
        axis=1,
    )
    window = (me - KWIN) * rows + jnp.arange((KWIN + 1) * rows, dtype=jnp.int32)
    rec = jnp.sum((window[:, None] >= ends[None, :]).astype(jnp.int32), axis=1)
    own_pos, own_rec = window[KWIN * rows :], rec[KWIN * rows :]
    listed = jnp.any(block_lists[0][None, :] == (window // rows)[:, None], axis=1) & (window >= 0)
    allowed = (
        listed[None, :]
        & (rec[None, :] == own_rec[:, None])
        & (window[None, :] <= own_pos[:, None])
    )
    bias = jnp.where(allowed, 0.0, -1e30).astype(F32)
    same = jnp.where(
        (own_pos[:, None] >= own_pos[None, :]) & (own_rec[:, None] == own_rec[None, :]), 0.0, -1e30
    ).astype(F32)

    tri = (jnp.arange(rows)[:, None] <= jnp.arange(rows)[None, :]).astype(F32)
    cum = jnp.dot(log_decay, tri, precision=HIGH)
    first_keep = jnp.where(jnp.any(ends == own_pos[0]) | (own_pos[0] == 0), 0.0, 1.0)
    enter = jnp.exp(cum) * (first_keep * (own_rec == own_rec[0]).astype(F32))
    leave = jnp.exp(cum[:, -1:] - cum) * (own_rec == own_rec[-1]).astype(F32)
    through = enter[:, -1]
    leave_wide = jnp.repeat(leave.T, size, axis=1)
    enter_wide = jnp.repeat(enter.T, size, axis=1)
    xl = (ssm_input.astype(F32) * leave_wide).astype(BF16)
    de = (out_grad.astype(F32) * enter_wide).astype(BF16)
    pushed = dot(xl, state_write, TN).astype(BF16)
    pulled = dot(de, state_read, TN).astype(BF16)
    coarse = lax.reduce_precision(through, 8, 7)
    fine = lax.reduce_precision(through - coarse, 8, 7)
    tail = jnp.zeros((16, states), F32).at[0, :heads].set(coarse).at[1, :heads].set(fine)
    packed = jnp.concatenate([pushed, pulled, tail.astype(BF16)], axis=0)
    gathered = lax.all_gather(packed, "seq")

    vmem = pl.BlockSpec(memory_space=pltpu.VMEM)
    wide = jax.ShapeDtypeStruct((rows, width), BF16)
    gq, gk, gv, gxi, gbi, gci, gli = pl.pallas_call(
        functools.partial(mix_kernel, count, heads),
        out_shape=(
            wide,
            wide,
            wide,
            jax.ShapeDtypeStruct((rows, width), F32),
            jax.ShapeDtypeStruct((rows, states), F32),
            jax.ShapeDtypeStruct((rows, states), F32),
            jax.ShapeDtypeStruct((rows, lanes), F32),
        ),
        in_specs=[vmem] * 11,
        out_specs=(vmem,) * 7,
        scratch_shapes=[pltpu.VMEM(((KWIN + 1) * rows, width), BF16)] * 4
        + [pltpu.VMEM((KWIN, rows, width), BF16)] * 2
        + [pltpu.VMEM((rows, rows), F32)]
        + [pltpu.SemaphoreType.DMA((KWIN, 2))] * 4,
        compiler_params=pltpu.CompilerParams(
            collective_id=0, has_side_effects=True, vmem_limit_bytes=40 * 2**20
        ),
        cost_estimate=pl.CostEstimate(
            flops=10**10, bytes_accessed=3 * 10**7, transcendentals=10**6
        ),
    )(
        queries,
        key_rows,
        value_rows,
        out_grad,
        ssm_input,
        state_write,
        state_read,
        bias,
        same,
        cum,
        cum.T,
    )

    each = gathered[:, 2 * width, :heads].astype(F32) + gathered[:, 2 * width + 1, :heads].astype(
        F32
    )
    ids = jnp.arange(count)
    src, mid = ids[:, None], ids[None, :]
    between_f = (mid > src) & (mid < me)
    between_b = (mid < src) & (mid > me)
    weight_f = jnp.prod(jnp.where(between_f[:, :, None], each[None], 1.0), axis=1)
    weight_b = jnp.prod(jnp.where(between_b[:, :, None], each[None], 1.0), axis=1)
    weight_f = jnp.where((ids < me)[:, None], weight_f, 0.0)
    weight_b = jnp.where((ids > me)[:, None], weight_b, 0.0)
    parts = gathered[:, : 2 * width].reshape(count, 2, heads, size, states).astype(F32)
    weights = jnp.stack([weight_f, weight_b], axis=1)[..., None, None]
    joined = jnp.sum(parts * weights, axis=0).reshape(2, width, states)

    grad_input, grad_write, grad_read, grad_l = pl.pallas_call(
        functools.partial(join_kernel, heads),
        out_shape=(
            wide,
            jax.ShapeDtypeStruct((rows, states), BF16),
            jax.ShapeDtypeStruct((rows, states), BF16),
            jax.ShapeDtypeStruct((rows, lanes), F32),
        ),
        in_specs=[vmem] * 12,
        out_specs=(vmem,) * 4,
        compiler_params=pltpu.CompilerParams(vmem_limit_bytes=40 * 2**20),
    )(
        joined[0],
        joined[1],
        xl,
        de,
        leave_wide,
        state_write,
        state_read,
        jnp.pad(through, (0, lanes - heads))[None],
        gxi,
        gbi,
        gci,
        gli,
    )
    return (gq, gk, gv, grad_input, grad_write, grad_read, grad_l[:, :heads].T)


def solution(mesh):
    rows = P(("grp", "seq"), None)
    turned = P(None, ("grp", "seq"))
    return jax.shard_map(
        body,
        mesh=mesh,
        in_specs=(rows,) * 7 + (turned, rows, P("grp")),
        out_specs=(rows,) * 6 + (turned,),
        check_vma=False,
    )
```

time: 235 us -> 142 us (0.60)
  Pallas kernels: 0 us -> 100 us
  local copies, waits for them, and re-layouts: 61.9 us -> 5.58 us
  starting transfers between devices: 36.8 us -> 0.04 us
  waiting for transfers between devices: 35.4 us -> 0.04 us
  matrix products: 36.2 us -> 2.11 us
  blocking collectives: 25.9 us -> 0 us
    pallas_call x0 -> x2, Pallas kernels: none -> 100 us  [the longest x1 98.3 us: body(): pl.pallas_call(functools.partial(mix_kernel, count, heads), out_shape=(wi...]
    ppermute x16 -> x0, starting transfers between devices: 36.7 us -> none  [passed_along(): return lax.ppermute(block, axis, route)]
    ppermute x16 -> x0, waiting for transfers between devices: 35.3 us -> none  [passed_along(): return lax.ppermute(block, axis, route)]
    dot_general x24 -> x3, matrix products: 29.7 us -> 2.11 us  [the longest x2 1.99 us: dot(): lax.dot_general(a, b, (dims, ((), ())), precision=precision, preferred_el...]
    all_gather x1 -> x0, blocking collectives: 25.9 us -> none  [carried_in(): gathered = jax.tree.map(lambda a: lax.all_gather(a, axis), part)]
    dynamic_slice x30 -> x0, local copies, waits for them, and re-layouts: 19.4 us -> none  [one(): lax.dynamic_index_in_dim(a, source, 0, False)]
    mul x15 -> x2, local copies, waits for them, and re-layouts: 10.3 us -> 0.23 us  [body(): joined = jnp.sum(parts * weights, axis=0).reshape(2, width, states)]
    reshape x4 -> x2, local copies, waits for them, and re-layouts: 8.81 us -> 0.33 us  [the longest x1 0.16 us: body(): enter_wide = jnp.repeat(enter.T, size, axis=1)]
  transfers between devices with their start and end apart: 18 -> 1, of which waited for: 7 -> 0; matrix products, arithmetic and copies ran while one was open for 41% -> 1% of each run, Pallas kernels for 0% -> 70%
where the time goes in v1:
time: 142 us; the launch traced here: 140 us
  Pallas kernels  100 us (70%)
  other arithmetic  16.7 us (12%)
  between operations  15.7 us (11%)
  local copies, waits for them, and re-layouts  5.58 us (4%)
  matrix products  2.11 us (1%)
    pallas_call x1, Pallas kernels, body(): pl.pallas_call(functools.partial(mix_kernel, count, heads), out_shape=(wi...  98.3 us
    reduce_sum x1, other arithmetic, body(): joined = jnp.sum(parts * weights, axis=0).reshape(2, width, states)  7.21 us
  transfers between devices with their start and end apart: 1, of which 0 were waited for; matrix products, arithmetic and copies ran while one was open for 1% of the time, Pallas kernels for 70%

profile of v1, /device:TPU:3, one launch (start us, length us, event | category | flops | bytes accessed | tf_op | source)
XLA Modules:
  0.0 140.2 jit_solution(3876792269476202853)
XLA Ops:
  7.3 0.5 slice.87
  7.8 0.8 select_reduce_fusion.2
  8.7 1.3 compare_reduce_fusion.1
  10.6 0.6 fusion.11
  11.9 0.7 compare_select_fusion
  12.5 0.6 slice.97
  13.1 0.1 fusion
  13.2 0.7 compare_convert_fusion
  13.9 0.8 slice_reduce_fusion
  14.9 0.2 copy.27.leave_ref
  15.1 0.2 copy.28
  15.3 1.0 multiply_convert_fusion.1.xl_ref
  16.3 1.0 convolution_convert_fusion.1
  17.3 1.0 multiply_convert_fusion.de_ref
  18.2 1.0 convolution_convert_fusion
  19.2 0.2 scatter.9
  19.4 0.8 pad_maximum_fusion
  20.2 0.1 copy.26.cum_t_ref
  20.4 0.7 compare_reduce_fusion
  21.1 0.1 and_select_fusion.1.same_ref
  21.2 0.2 and_select_fusion.bias_ref
  21.4 98.3 %shard_map.153 = (bf16[128,768]{1,0:T(8,128)(2,1)S(1)}, bf16[128,768]{1,0:T(8,128)(2,1)S(1)}, bf16[128,768]{1,0:T(8,128)(2,1)S(1)}, f32[128,768]{1,0:T(8,128)S(1...) custom-call(bf16[128,768]{1,0:T(8,128)(2,1)S(1)} %copy-done.5, ...), custom_call_target="tpu_custom_call" | custom-call | flops 10000000000 | bytes 30000000 | tf_op jit(solution)/shard_map/pallas_call | solution.py:336
  119.8 0.8 fusion.1
  120.8 0.5 select_reduce_fusion.1
  121.4 0.1 mul.61
  121.5 0.1 mul.62
  121.6 7.2 %multiply_reduce_fusion = f32[1536,128]{1,0:T(8,128)S(1)} fusion(bf16[16,1552,128]{2,1,0:T(8,128)(2,1)} %bitcast.32, f32[16,1536]{1,0:T(8,128)S(1)} %mul.62), kind=kLoop, calls=%fused_computation | loop fusion | flops 9240576 | bytes 7176192 | tf_op jit(solution)/shard_map/reduce_sum | solution.py:386
  128.9 1.8 %shard_map.154 = (bf16[128,768]{1,0:T(8,128)(2,1)}, bf16[128,128]{1,0:T(8,128)(2,1)}, bf16[128,128]{1,0:T(8,128)(2,1)}, f32[128,128]{1,0:T(8,128)S(1)}) custom-call(f32[768,128]{1,0:T(8,128)S(1)} %get-tuple-element.79.state_ref, f32[768,128]{1,0:T(8,128)S(1)} %get-tuple-element.78.grad_ref, bf16[128,768]{1,0:T(8,128)(2,1)S(1)} %multiply_convert_fusion.1.xl_ref, ...), custom_call_target="tpu_custom_call" | custom-call | tf_op jit(solution)/shard_map/pallas_call | solution.py:388
  130.7 0.7 copy.32
  131.4 0.7 copy.37
  132.1 0.7 copy.38
  132.7 0.7 copy.39
  (40 shorter events, 0.7 us)
Async XLA Ops:
  7.2 5.9 %copy-start = (f32[12,128]{1,0:T(8,128)S(1)}, f32[12,128]{1,0:T(8,128)}, u32[]{:S(2)}) copy-start(f32[12,128]{1,0:T(8,128)} %param.21) | copy-start | bytes 18436
  7.2 14.2 %copy-start.2 = (bf16[128,768]{1,0:T(8,128)(2,1)S(1)}, bf16[128,768]{1,0:T(8,128)(2,1)}, u32[]{:S(2)}) copy-start(bf16[128,768]{1,0:T(8,128)(2,1)} %x_ref.1) | copy-start | bytes 589828
  7.2 14.2 %copy-start.3 = (bf16[128,128]{1,0:T(8,128)(2,1)S(1)}, bf16[128,128]{1,0:T(8,128)(2,1)}, u32[]{:S(2)}) copy-start(bf16[128,128]{1,0:T(8,128)(2,1)} %b_ref.3) | copy-start | bytes 98308
  7.2 14.2 %copy-start.1 = (bf16[128,768]{1,0:T(8,128)(2,1)S(1)}, bf16[128,768]{1,0:T(8,128)(2,1)}, u32[]{:S(2)}) copy-start(bf16[128,768]{1,0:T(8,128)(2,1)} %do_ref.1) | copy-start | bytes 589828
  7.2 14.2 %copy-start.4 = (bf16[128,128]{1,0:T(8,128)(2,1)S(1)}, bf16[128,128]{1,0:T(8,128)(2,1)}, u32[]{:S(2)}) copy-start(bf16[128,128]{1,0:T(8,128)(2,1)} %c_ref.3) | copy-start | bytes 98308
  7.2 14.2 %copy-start.5 = (bf16[128,768]{1,0:T(8,128)(2,1)S(1)}, bf16[128,768]{1,0:T(8,128)(2,1)}, u32[]{:S(2)}) copy-start(bf16[128,768]{1,0:T(8,128)(2,1)} %q_ref.1) | copy-start | bytes 589828
  7.2 14.2 %copy-start.6 = (bf16[128,768]{1,0:T(8,128)(2,1)S(1)}, bf16[128,768]{1,0:T(8,128)(2,1)}, u32[]{:S(2)}) copy-start(bf16[128,768]{1,0:T(8,128)(2,1)} %k_ref.1) | copy-start | bytes 589828
  7.3 14.2 %copy-start.7 = (bf16[128,768]{1,0:T(8,128)(2,1)S(1)}, bf16[128,768]{1,0:T(8,128)(2,1)}, u32[]{:S(2)}) copy-start(bf16[128,768]{1,0:T(8,128)(2,1)} %v_ref.1) | copy-start | bytes 589828
  7.3 112.6 %all-gather.3.cloned.1.call-start = ((), (), s32[]{:S(2)}) async-start(), calls=%async_computation | async-start | bytes 6754304 | tf_op jit(solution)/shard_map/all_gather | solution.py:332
Sparse Core Ops, SparseCore 0:
  20.3 78.7 all-gather.2

commit v2 on v1

--- a/solution.py
+++ b/solution.py
@@ -8,6 +8,7 @@
 from jax.sharding import PartitionSpec as P
 
 KWIN = 4
+PARTS = 2
 F32 = jnp.float32
 BF16 = jnp.bfloat16
 HIGH = lax.Precision.HIGHEST
@@ -50,6 +51,7 @@
     rk,
     rv,
     wsum,
+    total,
     send_sem,
     recv_sem,
     bsend_sem,
@@ -59,79 +61,90 @@
     rows, width = q_ref.shape
     size = width // heads
     scale = size ** (-0.5)
-    own = KWIN * rows
-
-    def place(dist):
-        return pl.ds((KWIN - dist) * rows, rows)
-
-    def forward(dist):
-        return [
-            pltpu.make_async_remote_copy(
-                src_ref=src,
-                dst_ref=dst.at[place(dist), :],
-                send_sem=send_sem.at[dist - 1, i],
-                recv_sem=recv_sem.at[dist - 1, i],
-                device_id={"seq": me + dist},
-                device_id_type=pl.DeviceIdType.MESH,
-            )
-            for i, (src, dst) in enumerate(((k_ref, kw), (v_ref, vw)))
-        ]
-
-    def backward(dist):
-        return [
-            pltpu.make_async_remote_copy(
-                src_ref=src.at[place(dist), :],
-                dst_ref=dst.at[dist - 1],
-                send_sem=bsend_sem.at[dist - 1, i],
-                recv_sem=brecv_sem.at[dist - 1, i],
-                device_id={"seq": me - dist},
-                device_id_type=pl.DeviceIdType.MESH,
-            )
-            for i, (src, dst) in enumerate(((pk, rk), (pv, rv)))
-        ]
+    odd = lax.rem(me, 2)
+    side = lax.div(lax.rem(me, KWIN), 2)
+    mate = me + 1 - 2 * odd
+    across = me + 2 - 4 * side
+    part = width // PARTS
+
+    def place(slot):
+        return pl.ds(pl.multiple_of((KWIN - slot) * rows, rows), rows)
+
+    routes = (
+        (0, KWIN, me + KWIN),
+        (KWIN * side, 2, across),
+        (KWIN * odd, 1 + 2 * odd, mate),
+        (2, 3 - 2 * odd, mate),
+    )
+
+    def forward(hop, i):
+        src, dst, device = routes[hop]
+        ref = (kw, vw)[i]
+        return pltpu.make_async_remote_copy(
+            src_ref=ref.at[place(src), :],
+            dst_ref=ref.at[place(dst), :],
+            send_sem=send_sem.at[hop, i],
+            recv_sem=recv_sem.at[hop, i],
+            device_id={"seq": device},
+            device_id_type=pl.DeviceIdType.MESH,
+        )
+
+    backs = ((KWIN, me - KWIN), (2, across), (3 - 2 * odd, mate), (1 + 2 * odd, mate))
+
+    def backward(hop, i, c):
+        src, device = backs[hop]
+        cols = pl.ds(c * part, part)
+        return pltpu.make_async_remote_copy(
+            src_ref=(pk, pv)[i].at[place(src), cols],
+            dst_ref=(rk, rv)[i].at[hop, :, cols],
+            send_sem=bsend_sem.at[hop, i * PARTS + c],
+            recv_sem=brecv_sem.at[hop, i * PARTS + c],
+            device_id={"seq": device},
+            device_id_type=pl.DeviceIdType.MESH,
+        )
 
     barrier = pltpu.get_barrier_semaphore()
-    for dist in range(1, KWIN + 1):
-
-        @pl.when(me + dist < count)
-        def _():
-            pl.semaphore_signal(
-                barrier, inc=1, device_id={"seq": me + dist}, device_id_type=pl.DeviceIdType.MESH
-            )
-
-        @pl.when(me - dist >= 0)
-        def _():
-            pl.semaphore_signal(
-                barrier, inc=1, device_id={"seq": me - dist}, device_id_type=pl.DeviceIdType.MESH
-            )
-
-    peers = 0
-    for dist in range(1, KWIN + 1):
-        peers += (me + dist < count).astype(jnp.int32) + (me - dist >= 0).astype(jnp.int32)
+    for device in (mate, across):
+        pl.semaphore_signal(
+            barrier, inc=1, device_id={"seq": device}, device_id_type=pl.DeviceIdType.MESH
+        )
+
+    @pl.when(me + KWIN < count)
+    def _():
+        pl.semaphore_signal(
+            barrier, inc=1, device_id={"seq": me + KWIN}, device_id_type=pl.DeviceIdType.MESH
+        )
+
+    @pl.when(me - KWIN >= 0)
+    def _():
+        pl.semaphore_signal(
+            barrier, inc=1, device_id={"seq": me - KWIN}, device_id_type=pl.DeviceIdType.MESH
+        )
+
+    kw[place(0), :] = k_ref[...]
+    vw[place(0), :] = v_ref[...]
+
+    @pl.when(me < KWIN)
+    def _():
+        kw[place(KWIN), :] = jnp.zeros((rows, width), BF16)
+        vw[place(KWIN), :] = jnp.zeros((rows, width), BF16)
+
+    peers = 2 + (me + KWIN < count).astype(jnp.int32) + (me - KWIN >= 0).astype(jnp.int32)
     pl.semaphore_wait(barrier, peers)
 
-    for dist in range(KWIN, 0, -1):
-
-        @pl.when(me + dist < count)
-        def _():
-            for copy in forward(dist):
-                copy.start()
-
-    zero = jnp.zeros((rows, width), BF16)
-    for dist in range(1, KWIN + 1):
-
-        @pl.when(me - dist < 0)
-        def _():
-            kw[place(dist), :] = zero
-            vw[place(dist), :] = zero
-
-        @pl.when(me + dist >= count)
-        def _():
-            rk[dist - 1] = zero
-            rv[dist - 1] = zero
-
-    kw[pl.ds(own, rows), :] = k_ref[...]
-    vw[pl.ds(own, rows), :] = v_ref[...]
+    for i in range(2):
+
+        @pl.when(me + KWIN < count)
+        def _():
+            forward(0, i).start()
+
+        @pl.when(side == 0)
+        def _():
+            forward(1, i).start()
+
+        @pl.when(odd == 0)
+        def _():
+            forward(2, i).start()
 
     cross = dot(c_ref[...], b_ref[...], NT)
     row_id = lax.broadcasted_iota(jnp.int32, (rows, rows), 0)
@@ -165,12 +178,26 @@
     gc_ref[...] = dot(weighted, b_ref[...], NN)
     gb_ref[...] = dot(weighted, c_ref[...], TN)
 
-    for dist in range(1, KWIN + 1):
-
-        @pl.when(me - dist >= 0)
-        def _():
-            for copy in forward(dist):
-                copy.wait_recv()
+    for i in range(2):
+
+        @pl.when(me - KWIN >= 0)
+        def _():
+            forward(0, i).wait_recv()
+
+        @pl.when(side == 1)
+        def _():
+            forward(1, i).start()
+
+        @pl.when(odd == 1)
+        def _():
+            forward(2, i).start()
+
+    for i in range(2):
+        forward(1, i).wait_recv()
+        forward(3, i).start()
+    for i in range(2):
+        forward(2, i).wait_recv()
+        forward(3, i).wait_recv()
 
     def pair_of_heads(step, carry):
         cols = pl.ds(pl.multiple_of(step * 2 * size, 2 * size), 2 * size)
@@ -193,38 +220,75 @@
         pv[:, cols] = jnp.concatenate(gv, axis=1).astype(BF16)
         return carry
 
-    lax.fori_loop(0, heads // 2, pair_of_heads, 0)
-
-    for dist in range(KWIN, 0, -1):
-
-        @pl.when(me - dist >= 0)
-        def _():
-            for copy in backward(dist):
-                copy.start()
-
-    for dist in range(1, KWIN + 1):
-
-        @pl.when(me + dist < count)
-        def _():
-            for copy in forward(dist):
-                copy.wait_send()
-            for copy in backward(dist):
-                copy.wait_recv()
-
-    total_k = pk[pl.ds(own, rows), :].astype(F32)
-    total_v = pv[pl.ds(own, rows), :].astype(F32)
-    for dist in range(1, KWIN + 1):
-        total_k = total_k + rk[dist - 1].astype(F32)
-        total_v = total_v + rv[dist - 1].astype(F32)
-    gk_ref[...] = total_k.astype(BF16)
-    gv_ref[...] = total_v.astype(BF16)
-
-    for dist in range(1, KWIN + 1):
-
-        @pl.when(me - dist >= 0)
-        def _():
-            for copy in backward(dist):
-                copy.wait_send()
+    def add(i, c, slot, hop):
+        cols = pl.ds(c * part, part)
+        ref, got = (pk, pv)[i], (rk, rv)[i]
+        ref[place(slot), cols] = (
+            ref[place(slot), cols].astype(F32) + got[hop, :, cols].astype(F32)
+        ).astype(BF16)
+
+    def pass_across(c):
+        for i in range(2):
+            backward(3, i, c).wait_recv()
+            add(i, c, 2, 3)
+            backward(1, i, c).start()
+
+    def pass_back(c):
+        for i in range(2):
+            backward(2, i, c).wait_recv()
+            backward(1, i, c).wait_recv()
+            cols = pl.ds(c * part, part)
+            ref, got = (pk, pv)[i], (rk, rv)[i]
+            near = got[2, :, cols].astype(F32)
+            far = got[1, :, cols].astype(F32)
+            near_own = (1 - odd).astype(F32)
+            far_own = (1 - side).astype(F32)
+            through = near * (1.0 - near_own) + far * (1.0 - far_own)
+            kept = near * near_own + far * far_own
+            ref[place(KWIN), cols] = (
+                ref[place(KWIN), cols].astype(F32) + through
+            ).astype(BF16)
+
+            @pl.when(me - KWIN >= 0)
+            def _():
+                backward(0, i, c).start()
+
+            total[i, :, cols] = ref[place(0), cols].astype(F32) + kept
+
+    pairs = heads // 2 // PARTS
+    for c in range(PARTS):
+        lax.fori_loop(c * pairs, (c + 1) * pairs, pair_of_heads, 0)
+        for hop in (3, 2):
+            for i in range(2):
+                backward(hop, i, c).start()
+        if c > 0:
+            pass_across(c - 1)
+    pass_across(PARTS - 1)
+    for c in range(PARTS):
+        pass_back(c)
+
+    for i in range(2):
+
+        @pl.when(me + KWIN < count)
+        def _():
+            forward(0, i).wait_send()
+            for c in range(PARTS):
+                cols = pl.ds(c * part, part)
+                backward(0, i, c).wait_recv()
+                total[i, :, cols] = total[i, :, cols] + (rk, rv)[i][0, :, cols].astype(F32)
+
+        for hop in range(1, KWIN):
+            forward(hop, i).wait_send()
+            for c in range(PARTS):
+                backward(hop, i, c).wait_send()
+
+        @pl.when(me - KWIN >= 0)
+        def _():
+            for c in range(PARTS):
+                backward(0, i, c).wait_send()
+
+    gk_ref[...] = total[0].astype(BF16)
+    gv_ref[...] = total[1].astype(BF16)
 
 
 def join_kernel(
@@ -348,8 +412,9 @@
         out_specs=(vmem,) * 7,
         scratch_shapes=[pltpu.VMEM(((KWIN + 1) * rows, width), BF16)] * 4
         + [pltpu.VMEM((KWIN, rows, width), BF16)] * 2
-        + [pltpu.VMEM((rows, rows), F32)]
-        + [pltpu.SemaphoreType.DMA((KWIN, 2))] * 4,
+        + [pltpu.VMEM((rows, rows), F32), pltpu.VMEM((2, rows, width), F32)]
+        + [pltpu.SemaphoreType.DMA((KWIN, 2))] * 2
+        + [pltpu.SemaphoreType.DMA((KWIN, 2 * PARTS))] * 2,
         compiler_params=pltpu.CompilerParams(
             collective_id=0, has_side_effects=True, vmem_limit_bytes=40 * 2**20
         ),

time: 142 us -> 114 us (0.80)
  Pallas kernels: 100 us -> 62.2 us
  waiting for transfers between devices: 0.04 us -> 11.1 us
    pallas_call x1, Pallas kernels: 98.3 us -> 60.4 us  [body(): pl.pallas_call(functools.partial(mix_kernel, count, heads), out_shape=(wi...]
    all_gather x1, waiting for transfers between devices: 0.02 us -> 11.1 us  [body(): gathered = lax.all_gather(packed, 'seq')]
  transfers between devices with their start and end apart: 1 -> 1, of which waited for: 0 -> 1; matrix products, arithmetic and copies ran while one was open for 1% -> 1% of each run, Pallas kernels for 70% -> 53%
where the time goes in v2:
time: 114 us; the launch traced here: 113 us
  Pallas kernels  62.2 us (55%)
  other arithmetic  16.7 us (15%)
  between operations  15.7 us (14%)
  waiting for transfers between devices  11.1 us (10%)
  local copies, waits for them, and re-layouts  5.58 us (5%)
  matrix products  2.11 us (2%)
    pallas_call x1, Pallas kernels, body(): pl.pallas_call(functools.partial(mix_kernel, count, heads), out_shape=(wi...  60.4 us
    all_gather x1, waiting for transfers between devices, body(): gathered = lax.all_gather(packed, 'seq')  11.1 us
    reduce_sum x1, other arithmetic, body(): joined = jnp.sum(parts * weights, axis=0).reshape(2, width, states)  7.21 us
    unnamed x20, local copies, waits for them, and re-layouts  2.75 us
  transfers between devices with their start and end apart: 1, of which 1 were waited for; matrix products, arithmetic and copies ran while one was open for 1% of the time, Pallas kernels for 53%

profile of v2, /device:TPU:3, one launch (start us, length us, event | category | flops | bytes accessed | tf_op | source)
XLA Modules:
  0.0 113.4 jit_solution(7071248725203641655)
XLA Ops:
  7.3 0.5 slice.87
  7.8 0.8 select_reduce_fusion.2
  8.7 1.3 %compare_reduce_fusion.1 = pred[]{:T(512)} fusion(s32[8]{0:T(128)S(1)} %select_reduce_fusion.2, s32[]{:T(128)} %bitcast.5), kind=kLoop, calls=%fused_computation.42 | loop fusion | flops 15 | bytes 37 | tf_op jit(solution)/shard_map/reduce_or | solution.py:382
  10.6 0.6 fusion.11
  11.9 0.7 compare_select_fusion
  12.5 0.6 slice.97
  13.1 0.1 fusion
  13.2 0.7 compare_convert_fusion
  13.9 0.8 slice_reduce_fusion
  14.9 0.2 copy.27.leave_ref
  15.1 0.2 copy.28
  15.3 1.0 multiply_convert_fusion.1.xl_ref
  16.3 1.0 convolution_convert_fusion.1
  17.3 1.0 multiply_convert_fusion.de_ref
  18.2 1.0 convolution_convert_fusion
  19.2 0.2 scatter.9
  19.4 0.8 pad_maximum_fusion
  20.2 0.1 copy.26.cum_t_ref
  20.4 0.7 compare_reduce_fusion
  21.2 0.2 and_select_fusion.bias_ref
  21.4 60.4 %shard_map.153 = (bf16[128,768]{1,0:T(8,128)(2,1)S(1)}, bf16[128,768]{1,0:T(8,128)(2,1)S(1)}, bf16[128,768]{1,0:T(8,128)(2,1)S(1)}, f32[128,768]{1,0:T(8,128)S(1...) custom-call(bf16[128,768]{1,0:T(8,128)(2,1)S(1)} %copy-done.5, ...), custom_call_target="tpu_custom_call" | custom-call | flops 10000000000 | bytes 30000000 | tf_op jit(solution)/shard_map/pallas_call | solution.py:400
  81.9 11.1 %all-gather.3.cloned.1.call-done = bf16[24832,128]{1,0:T(8,128)(2,1)} async-done(((bf16[1552,128]{1,0:T(8,128)(2,1)}), bf16[24832,128]{1,0:T(8,128)(2,1)}) %all-gather.3.cloned.1.call-update) | async-done | bytes 6357008 | tf_op jit(solution)/shard_map/all_gather | solution.py:396
  93.0 0.8 fusion.1
  93.9 0.5 select_reduce_fusion.1
  94.5 0.1 mul.61
  94.7 0.1 mul.62
  94.8 7.2 %multiply_reduce_fusion = f32[1536,128]{1,0:T(8,128)S(1)} fusion(bf16[16,1552,128]{2,1,0:T(8,128)(2,1)} %bitcast.32, f32[16,1536]{1,0:T(8,128)S(1)} %mul.62), kind=kLoop, calls=%fused_computation | loop fusion | flops 9240576 | bytes 7176192 | tf_op jit(solution)/shard_map/reduce_sum | solution.py:451
  102.0 1.8 %shard_map.154 = (bf16[128,768]{1,0:T(8,128)(2,1)}, bf16[128,128]{1,0:T(8,128)(2,1)}, bf16[128,128]{1,0:T(8,128)(2,1)}, f32[128,128]{1,0:T(8,128)S(1)}) custom-call(f32[768,128]{1,0:T(8,128)S(1)} %get-tuple-element.79.state_ref, f32[768,128]{1,0:T(8,128)S(1)} %get-tuple-element.78.grad_ref, bf16[128,768]{1,0:T(8,128)(2,1)S(1)} %multiply_convert_fusion.1.xl_ref, ...), custom_call_target="tpu_custom_call" | custom-call | tf_op jit(solution)/shard_map/pallas_call | solution.py:453
  103.8 0.7 copy.32
  104.5 0.7 copy.37
  105.2 0.7 copy.38
  105.9 0.7 copy.39
  (40 shorter events, 0.7 us)
Async XLA Ops:
  7.2 5.9 %copy-start = (f32[12,128]{1,0:T(8,128)S(1)}, f32[12,128]{1,0:T(8,128)}, u32[]{:S(2)}) copy-start(f32[12,128]{1,0:T(8,128)} %param.21) | copy-start | bytes 18436
  7.2 14.2 %copy-start.2 = (bf16[128,768]{1,0:T(8,128)(2,1)S(1)}, bf16[128,768]{1,0:T(8,128)(2,1)}, u32[]{:S(2)}) copy-start(bf16[128,768]{1,0:T(8,128)(2,1)} %x_ref.1) | copy-start | bytes 589828
  7.2 14.2 %copy-start.3 = (bf16[128,128]{1,0:T(8,128)(2,1)S(1)}, bf16[128,128]{1,0:T(8,128)(2,1)}, u32[]{:S(2)}) copy-start(bf16[128,128]{1,0:T(8,128)(2,1)} %b_ref.3) | copy-start | bytes 98308
  7.2 14.2 %copy-start.1 = (bf16[128,768]{1,0:T(8,128)(2,1)S(1)}, bf16[128,768]{1,0:T(8,128)(2,1)}, u32[]{:S(2)}) copy-start(bf16[128,768]{1,0:T(8,128)(2,1)} %do_ref.1) | copy-start | bytes 589828
  7.2 14.2 %copy-start.4 = (bf16[128,128]{1,0:T(8,128)(2,1)S(1)}, bf16[128,128]{1,0:T(8,128)(2,1)}, u32[]{:S(2)}) copy-start(bf16[128,128]{1,0:T(8,128)(2,1)} %c_ref.3) | copy-start | bytes 98308
  7.2 14.2 %copy-start.5 = (bf16[128,768]{1,0:T(8,128)(2,1)S(1)}, bf16[128,768]{1,0:T(8,128)(2,1)}, u32[]{:S(2)}) copy-start(bf16[128,768]{1,0:T(8,128)(2,1)} %q_ref.1) | copy-start | bytes 589828
  7.2 14.2 %copy-start.6 = (bf16[128,768]{1,0:T(8,128)(2,1)S(1)}, bf16[128,768]{1,0:T(8,128)(2,1)}, u32[]{:S(2)}) copy-start(bf16[128,768]{1,0:T(8,128)(2,1)} %k_ref.1) | copy-start | bytes 589828
  7.3 14.2 %copy-start.7 = (bf16[128,768]{1,0:T(8,128)(2,1)S(1)}, bf16[128,768]{1,0:T(8,128)(2,1)}, u32[]{:S(2)}) copy-start(bf16[128,768]{1,0:T(8,128)(2,1)} %v_ref.1) | copy-start | bytes 589828
  7.3 85.7 %all-gather.3.cloned.1.call-start = ((), (), s32[]{:S(2)}) async-start(), calls=%async_computation | async-start | bytes 6754304 | tf_op jit(solution)/shard_map/all_gather | solution.py:396
Sparse Core Ops, SparseCore 0:
  20.3 72.5 all-gather.2

commit v3 on v2

--- a/solution.py
+++ b/solution.py
@@ -37,6 +37,8 @@
     same_ref,
     cum_ref,
     cum_t_ref,
+    u_ref,
+    a_ref,
     gq_ref,
     gk_ref,
     gv_ref,
@@ -44,6 +46,7 @@
     gb_ref,
     gc_ref,
     gl_ref,
+    st_ref,
     kw,
     vw,
     pk,
@@ -52,6 +55,17 @@
     rv,
     wsum,
     total,
+    got_u,
+    got,
+    got_a,
+    duo,
+    pair_a,
+    chain,
+    chain_in,
+    plane_sum,
+    plane_a,
+    ssend_sem,
+    srecv_sem,
     send_sem,
     recv_sem,
     bsend_sem,
@@ -103,6 +117,44 @@
             device_id_type=pl.DeviceIdType.MESH,
         )
 
+    def state_copy(src, dst, device, level, i):
+        return pltpu.make_async_remote_copy(
+            src_ref=src,
+            dst_ref=dst,
+            send_sem=ssend_sem.at[level, i],
+            recv_sem=srecv_sem.at[level, i],
+            device_id={"seq": device},
+            device_id_type=pl.DeviceIdType.MESH,
+        )
+
+    def exchange(level):
+        src, src_a, device = ((u_ref, a_ref, mate), (duo, pair_a, across))[level]
+        return (
+            state_copy(src, (got_u, got)[level], device, level, 0),
+            state_copy(src_a, got_a.at[level], device, level, 1),
+        )
+
+    def chain_copy(i):
+        return state_copy(chain.at[i], chain_in.at[i], me + (KWIN, -KWIN)[i], 2, i)
+
+    last = lax.div(count - 1, KWIN)
+    plane = lax.div(me, KWIN)
+    away = (plane, last - plane)
+
+    def chain_step(i, now):
+        @pl.when(now)
+        def _():
+            @pl.when(away[i] > 0)
+            def _():
+                chain_copy(i).wait_recv()
+
+            @pl.when(away[1 - i] > 0)
+            def _():
+                chain[i] = (
+                    plane_sum[i] + plane_a[0, :1, :] * chain_in[i]
+                )
+                chain_copy(i).start()
+
     barrier = pltpu.get_barrier_semaphore()
     for device in (mate, across):
         pl.semaphore_signal(
@@ -131,6 +183,15 @@
 
     peers = 2 + (me + KWIN < count).astype(jnp.int32) + (me - KWIN >= 0).astype(jnp.int32)
     pl.semaphore_wait(barrier, peers)
+
+    for copy in exchange(0):
+        copy.start()
+
+    for i in range(2):
+
+        @pl.when(away[i] == 0)
+        def _():
+            chain_in[i] = jnp.zeros(chain_in.shape[1:], F32)
 
     for i in range(2):
 
@@ -178,6 +239,35 @@
     gc_ref[...] = dot(weighted, b_ref[...], NN)
     gb_ref[...] = dot(weighted, c_ref[...], TN)
 
+    def meet(own_u, own_w, own_a, level, bit):
+        other_u = (got_u, got)[level][0].astype(F32)
+        other_w = (got_u, got)[level][1].astype(F32)
+        other_a = got_a[level, :1, :]
+        later = bit.astype(F32)
+        first = 1.0 - later
+        sum_u = own_u * (later + first * other_a) + other_u * (first + later * own_a)
+        sum_w = own_w * (first + later * other_a) + other_w * (later + first * own_a)
+        return sum_u, sum_w, own_a * other_a, other_u, other_w, other_a, later, first
+
+    for copy in exchange(0):
+        copy.wait_recv()
+    sum_u, sum_w, sum_a, other_u, other_w, other_a, later, first_in = meet(
+        u_ref[0], u_ref[1], a_ref[:1, :], 0, odd
+    )
+    st_ref[0] = other_u * later
+    st_ref[1] = other_w * first_in
+    before_a = other_a * later + first_in
+    after_a = other_a * first_in + later
+    plane_sum[0] = sum_u
+    plane_sum[1] = sum_w
+    duo[0] = sum_u.astype(BF16)
+    duo[1] = sum_w.astype(BF16)
+    pair_a[...] = jnp.broadcast_to(sum_a, pair_a.shape)
+    plane_a[1] = jnp.broadcast_to(before_a, pair_a.shape)
+    plane_a[2] = jnp.broadcast_to(after_a, pair_a.shape)
+    for copy in exchange(1):
+        copy.start()
+
     for i in range(2):
 
         @pl.when(me - KWIN >= 0)
@@ -198,6 +288,21 @@
     for i in range(2):
         forward(2, i).wait_recv()
         forward(3, i).wait_recv()
+
+    for copy in exchange(1):
+        copy.wait_recv()
+    sum_u, sum_w, sum_a, other_u, other_w, other_a, later, first_in = meet(
+        plane_sum[0], plane_sum[1], pair_a[:1, :], 1, side
+    )
+    st_ref[0] = st_ref[0] + plane_a[1, :1, :] * later * other_u
+    st_ref[1] = st_ref[1] + plane_a[2, :1, :] * first_in * other_w
+    plane_a[1] = plane_a[1] * (other_a * later + first_in)
+    plane_a[2] = plane_a[2] * (other_a * first_in + later)
+    plane_a[0] = jnp.broadcast_to(sum_a, pair_a.shape)
+    plane_sum[0] = sum_u
+    plane_sum[1] = sum_w
+    for i in range(2):
+        chain_step(i, away[i] == 0)
 
     def pair_of_heads(step, carry):
         cols = pl.ds(pl.multiple_of(step * 2 * size, 2 * size), 2 * size)
@@ -263,9 +368,15 @@
                 backward(hop, i, c).start()
         if c > 0:
             pass_across(c - 1)
+        else:
+            for i in range(2):
+                chain_step(i, away[i] == 1)
     pass_across(PARTS - 1)
     for c in range(PARTS):
         pass_back(c)
+    for i in range(2):
+        chain_step(i, away[i] > 1)
+        st_ref[i] = st_ref[i] + plane_a[1 + i, :1, :] * chain_in[i]
 
     for i in range(2):
 
@@ -287,14 +398,22 @@
             for c in range(PARTS):
                 backward(0, i, c).wait_send()
 
+    for level in range(2):
+        for copy in exchange(level):
+            copy.wait_send()
+    for i in range(2):
+
+        @pl.when(away[1 - i] > 0)
+        def _():
+            chain_copy(i).wait_send()
+
     gk_ref[...] = total[0].astype(BF16)
     gv_ref[...] = total[1].astype(BF16)
 
 
 def join_kernel(
     heads,
-    state_ref,
-    grad_ref,
+    states_ref,
     xl_ref,
     de_ref,
     leave_ref,
@@ -313,13 +432,15 @@
     rows, width = gx_ref.shape
     size = width // heads
     lanes = gl_ref.shape[1]
-    state, grad = state_ref[...], grad_ref[...]
+    state, grad = states_ref[0], states_ref[1]
     state_b, grad_b = state.astype(BF16), grad.astype(BF16)
+    state_f = (state - state_b.astype(F32)).astype(BF16)
+    grad_f = (grad - grad_b.astype(F32)).astype(BF16)
     xl, de = xl_ref[...], de_ref[...]
-    gc_ref[...] = (gci_ref[...] + dot(de, state_b, NN)).astype(BF16)
-    gb_ref[...] = (gbi_ref[...] + dot(xl, grad_b, NN)).astype(BF16)
-    back = dot(b_ref[...], grad_b, NT)
-    ahead = dot(c_ref[...], state_b, NT)
+    gc_ref[...] = (gci_ref[...] + dot(de, state_b, NT) + dot(de, state_f, NT)).astype(BF16)
+    gb_ref[...] = (gbi_ref[...] + dot(xl, grad_b, NT) + dot(xl, grad_f, NT)).astype(BF16)
+    back = dot(b_ref[...], grad_b, NN) + dot(b_ref[...], grad_f, NN)
+    ahead = dot(c_ref[...], state_b, NN) + dot(c_ref[...], state_f, NN)
     gx_ref[...] = (gxi_ref[...] + leave_ref[...].astype(F32) * back).astype(BF16)
     owner = lax.broadcasted_iota(jnp.int32, (width, lanes), 0) // size
     pick = (owner == lax.broadcasted_iota(jnp.int32, (width, lanes), 1)).astype(F32)
@@ -329,7 +450,7 @@
     col_id = lax.broadcasted_iota(jnp.int32, (rows, rows), 1)
     later = dot((col_id >= row_id).astype(F32), from_start, NN, HIGH)
     earlier = dot((col_id < row_id).astype(F32), to_end, NN, HIGH)
-    each = dot(jnp.ones((8, state.shape[1]), F32), grad * state, NT, HIGH)
+    each = dot(jnp.ones((8, state.shape[0]), F32), grad * state, NN, HIGH)
     whole = dot(each, pick, NN, HIGH)[:1] * through_ref[...]
     gl_ref[...] = gli_ref[...] + later + earlier + whole
 
@@ -387,17 +508,12 @@
     enter_wide = jnp.repeat(enter.T, size, axis=1)
     xl = (ssm_input.astype(F32) * leave_wide).astype(BF16)
     de = (out_grad.astype(F32) * enter_wide).astype(BF16)
-    pushed = dot(xl, state_write, TN).astype(BF16)
-    pulled = dot(de, state_read, TN).astype(BF16)
-    coarse = lax.reduce_precision(through, 8, 7)
-    fine = lax.reduce_precision(through - coarse, 8, 7)
-    tail = jnp.zeros((16, states), F32).at[0, :heads].set(coarse).at[1, :heads].set(fine)
-    packed = jnp.concatenate([pushed, pulled, tail.astype(BF16)], axis=0)
-    gathered = lax.all_gather(packed, "seq")
+    ends_u = jnp.stack([dot(state_write, xl, TN), dot(state_read, de, TN)])
+    ends_a = jnp.broadcast_to(enter_wide[-1:], (8, width))
 
     vmem = pl.BlockSpec(memory_space=pltpu.VMEM)
     wide = jax.ShapeDtypeStruct((rows, width), BF16)
-    gq, gk, gv, gxi, gbi, gci, gli = pl.pallas_call(
+    gq, gk, gv, gxi, gbi, gci, gli, joined = pl.pallas_call(
         functools.partial(mix_kernel, count, heads),
         out_shape=(
             wide,
@@ -407,12 +523,25 @@
             jax.ShapeDtypeStruct((rows, states), F32),
             jax.ShapeDtypeStruct((rows, states), F32),
             jax.ShapeDtypeStruct((rows, lanes), F32),
+            jax.ShapeDtypeStruct((2, states, width), F32),
         ),
-        in_specs=[vmem] * 11,
-        out_specs=(vmem,) * 7,
+        in_specs=[vmem] * 13,
+        out_specs=(vmem,) * 8,
         scratch_shapes=[pltpu.VMEM(((KWIN + 1) * rows, width), BF16)] * 4
         + [pltpu.VMEM((KWIN, rows, width), BF16)] * 2
         + [pltpu.VMEM((rows, rows), F32), pltpu.VMEM((2, rows, width), F32)]
+        + [
+            pltpu.VMEM((2, states, width), F32),
+            pltpu.VMEM((2, states, width), BF16),
+            pltpu.VMEM((2, 8, width), F32),
+            pltpu.VMEM((2, states, width), BF16),
+            pltpu.VMEM((8, width), F32),
+            pltpu.VMEM((2, states, width), F32),
+            pltpu.VMEM((2, states, width), F32),
+            pltpu.VMEM((2, states, width), F32),
+            pltpu.VMEM((3, 8, width), F32),
+        ]
+        + [pltpu.SemaphoreType.DMA((3, 2))] * 2
         + [pltpu.SemaphoreType.DMA((KWIN, 2))] * 2
         + [pltpu.SemaphoreType.DMA((KWIN, 2 * PARTS))] * 2,
         compiler_params=pltpu.CompilerParams(
@@ -433,22 +562,9 @@
         same,
         cum,
         cum.T,
-    )
-
-    each = gathered[:, 2 * width, :heads].astype(F32) + gathered[:, 2 * width + 1, :heads].astype(
-        F32
-    )
-    ids = jnp.arange(count)
-    src, mid = ids[:, None], ids[None, :]
-    between_f = (mid > src) & (mid < me)
-    between_b = (mid < src) & (mid > me)
-    weight_f = jnp.prod(jnp.where(between_f[:, :, None], each[None], 1.0), axis=1)
-    weight_b = jnp.prod(jnp.where(between_b[:, :, None], each[None], 1.0), axis=1)
-    weight_f = jnp.where((ids < me)[:, None], weight_f, 0.0)
-    weight_b = jnp.where((ids > me)[:, None], weight_b, 0.0)
-    parts = gathered[:, : 2 * width].reshape(count, 2, heads, size, states).astype(F32)
-    weights = jnp.stack([weight_f, weight_b], axis=1)[..., None, None]
-    joined = jnp.sum(parts * weights, axis=0).reshape(2, width, states)
+        ends_u,
+        ends_a,
+    )
 
     grad_input, grad_write, grad_read, grad_l = pl.pallas_call(
         functools.partial(join_kernel, heads),
@@ -458,12 +574,11 @@
             jax.ShapeDtypeStruct((rows, states), BF16),
             jax.ShapeDtypeStruct((rows, lanes), F32),
         ),
-        in_specs=[vmem] * 12,
+        in_specs=[vmem] * 11,
         out_specs=(vmem,) * 4,
         compiler_params=pltpu.CompilerParams(vmem_limit_bytes=40 * 2**20),
     )(
-        joined[0],
-        joined[1],
+        joined,
         xl,
         de,
         leave_wide,

time: 114 us -> 82.9 us (0.73)
  between operations: 15.7 us -> 2.15 us
  other arithmetic: 16.7 us -> 4.24 us
  waiting for transfers between devices: 11.1 us -> 0 us
  local copies, waits for them, and re-layouts: 5.58 us -> 10.3 us
  Pallas kernels: 62.2 us -> 64.2 us
  matrix products: 2.11 us -> 0.63 us
    all_gather x1 -> x0, waiting for transfers between devices: 11.1 us -> none  [body(): gathered = lax.all_gather(packed, 'seq')]
    reduce_sum x1 -> x0, other arithmetic: 7.21 us -> none  [body(): joined = jnp.sum(parts * weights, axis=0).reshape(2, width, states)]
    unnamed x20 -> x24, local copies, waits for them, and re-layouts: 2.75 us -> 7.74 us
    pallas_call x1, Pallas kernels: 60.4 us -> 62.1 us  [body(): pl.pallas_call(functools.partial(mix_kernel, count, heads), out_shape=(wi...]
    dot_general x2, matrix products: 1.99 us -> 0.51 us  [dot(): lax.dot_general(a, b, (dims, ((), ())), precision=precision, preferred_el...]
  transfers between devices with their start and end apart: 1 -> 0, of which waited for: 1 -> 0; matrix products, arithmetic and copies ran while one was open for 1% -> 0% of each run, Pallas kernels for 53% -> 0%
where the time goes in v3:
time: 82.9 us; the launch traced here: 81.5 us
  Pallas kernels  64.2 us (77%)
  local copies, waits for them, and re-layouts  10.3 us (12%)
  other arithmetic  4.24 us (5%)
  between operations  2.15 us (3%)
    pallas_call x1, Pallas kernels, body(): pl.pallas_call(functools.partial(mix_kernel, count, heads), out_shape=(wi...  62.1 us
    unnamed x24, local copies, waits for them, and re-layouts  7.74 us
    pallas_call x1, Pallas kernels, body(): pl.pallas_call(functools.partial(join_kernel, heads), out_shape=(wide, ja...  2.07 us

profile of v3, /device:TPU:3, one launch (start us, length us, event | category | flops | bytes accessed | tf_op | source)
XLA Modules:
  0.0 81.5 jit_solution(7086027414856244296)
XLA Ops:
  0.7 0.6 copy-done.9
  1.3 0.1 select_reduce_fusion
  1.4 0.1 fusion
  1.6 0.5 slice.40
  2.8 1.3 %compare_reduce_fusion.1 = pred[]{:T(512)} fusion(s32[8]{0:T(128)S(1)} %select_reduce_fusion, s32[]{:T(128)} %bitcast.7), kind=kLoop, calls=%fused_computation.30 | loop fusion | flops 15 | bytes 37 | tf_op jit(solution)/shard_map/reduce_or | solution.py:503
  4.7 0.6 copy-done.8
  5.6 0.6 fusion.6
  6.1 0.6 compare_select_fusion
  6.8 0.6 slice.48
  7.4 0.6 compare_convert_fusion
  8.0 0.8 %multiply_reduce_fusion = (f32[12]{0:T(128)S(1)}, f32[12]{0:T(128)S(1)}) fusion(f32[12,128]{1,0:T(8,128)S(1)} %bitcast.24, f32[1]{0:T(128)} %slice.48), kind=kLoop, calls=%fused_computation.13 | loop fusion | flops 12 | bytes 148 | tf_op jit(solution)/shard_map/slice | solution.py:506
  9.0 0.2 slice_reduce_fusion
  9.3 0.1 and_select_fusion.1.same_ref
  9.4 0.1 copy.34.cum_t_ref
  9.5 0.2 and_select_fusion.bias_ref
  9.7 0.2 copy.32
  9.9 0.7 copy-done.1
  10.7 0.2 copy.30.leave_ref
  10.9 0.7 copy-done.2
  11.7 0.7 copy-done.3
  12.4 0.3 convolution_bitcast_fusion.1
  12.7 0.5 copy-done.4
  13.2 0.3 convolution_bitcast_fusion
  13.6 0.8 copy-done.5
  14.4 0.1 copy-done.6
  14.5 0.1 copy-done.7
  14.6 62.1 %shard_map.153 = (bf16[128,768]{1,0:T(8,128)(2,1)S(1)}, bf16[128,768]{1,0:T(8,128)(2,1)S(1)}, bf16[128,768]{1,0:T(8,128)(2,1)S(1)}, f32[128,768]{1,0:T(8,128)S(1...) custom-call(bf16[128,768]{1,0:T(8,128)(2,1)S(1)} %copy-done.5, ...), custom_call_target="tpu_custom_call" | custom-call | flops 10000000000 | bytes 30000000 | tf_op jit(solution)/shard_map/pallas_call | solution.py:516
  76.7 2.1 %shard_map.154 = (bf16[128,768]{1,0:T(8,128)(2,1)}, bf16[128,128]{1,0:T(8,128)(2,1)}, bf16[128,128]{1,0:T(8,128)(2,1)}, f32[128,128]{1,0:T(8,128)S(1)}) custom-call(f32[2,128,768]{2,1,0:T(8,128)S(1)} %get-tuple-element.22.states_ref, bf16[128,768]{1,0:T(8,128)(2,1)S(1)} %multiply_convert_fusion.1.xl_ref, bf16[128,768]{1,0:T(8,128)(2,1)S(1)} %multiply_convert_fusion.de_ref, ...), custom_call_target="tpu_custom_call" | custom-call | tf_op jit(solution)/shard_map/pallas_call | solution.py:569
  78.8 0.7 copy.36
  79.5 0.7 copy.42
  80.2 0.7 copy.43
  80.8 0.7 copy.44
  (28 shorter events, 0.7 us)
Async XLA Ops:
  0.6 0.8 copy-start
  0.7 0.7 copy-start.9
  4.7 0.7 copy-start.8
  9.7 0.9 %copy-start.1 = (bf16[128,768]{1,0:T(8,128)(2,1)S(1)}, bf16[128,768]{1,0:T(8,128)(2,1)}, u32[]{:S(2)}) copy-start(bf16[128,768]{1,0:T(8,128)(2,1)} %do_ref.1) | copy-start | bytes 589828
  10.7 0.9 %copy-start.2 = (bf16[128,768]{1,0:T(8,128)(2,1)S(1)}, bf16[128,768]{1,0:T(8,128)(2,1)}, u32[]{:S(2)}) copy-start(bf16[128,768]{1,0:T(8,128)(2,1)} %x_ref.1) | copy-start | bytes 589828
  11.7 0.8 copy-start.3
  12.4 0.8 copy-start.4
  13.4 0.9 %copy-start.5 = (bf16[128,768]{1,0:T(8,128)(2,1)S(1)}, bf16[128,768]{1,0:T(8,128)(2,1)}, u32[]{:S(2)}) copy-start(bf16[128,768]{1,0:T(8,128)(2,1)} %q_ref.1) | copy-start | bytes 589828
  13.5 1.0 %copy-start.6 = (bf16[128,768]{1,0:T(8,128)(2,1)S(1)}, bf16[128,768]{1,0:T(8,128)(2,1)}, u32[]{:S(2)}) copy-start(bf16[128,768]{1,0:T(8,128)(2,1)} %k_ref.1) | copy-start | bytes 589828
  13.5 1.1 %copy-start.7 = (bf16[128,768]{1,0:T(8,128)(2,1)S(1)}, bf16[128,768]{1,0:T(8,128)(2,1)}, u32[]{:S(2)}) copy-start(bf16[128,768]{1,0:T(8,128)(2,1)} %v_ref.1) | copy-start | bytes 589828

commit v4 on v3

--- a/solution.py
+++ b/solution.py
@@ -8,7 +8,7 @@
 from jax.sharding import PartitionSpec as P
 
 KWIN = 4
-PARTS = 2
+PARTS = 3
 F32 = jnp.float32
 BF16 = jnp.bfloat16
 HIGH = lax.Precision.HIGHEST

time: 82.9 us -> 83.5 us (level)
  the two profiles are of different devices: /device:TPU:3 before, /device:TPU:0 now
where the time goes in v4:
time: 83.5 us; the launch traced here: 83.1 us
  Pallas kernels  65.8 us (79%)
  local copies, waits for them, and re-layouts  10.3 us (12%)
  other arithmetic  4.24 us (5%)
  between operations  2.15 us (3%)
    pallas_call x1, Pallas kernels, body(): pl.pallas_call(functools.partial(mix_kernel, count, heads), out_shape=(wi...  63.8 us
    unnamed x24, local copies, waits for them, and re-layouts  7.74 us
    pallas_call x1, Pallas kernels, body(): pl.pallas_call(functools.partial(join_kernel, heads), out_shape=(wide, ja...  2.07 us

profile of v4, /device:TPU:0, one launch (start us, length us, event | category | flops | bytes accessed | tf_op | source)
XLA Modules:
  0.0 83.1 jit_solution(15726996632668940113)
XLA Ops:
  0.7 0.6 copy-done.9
  1.3 0.1 select_reduce_fusion
  1.4 0.1 fusion
  1.6 0.5 slice.40
  2.8 1.3 %compare_reduce_fusion.1 = pred[]{:T(512)} fusion(s32[8]{0:T(128)S(1)} %select_reduce_fusion, s32[]{:T(128)} %bitcast.7), kind=kLoop, calls=%fused_computation.30 | loop fusion | flops 15 | bytes 37 | tf_op jit(solution)/shard_map/reduce_or | solution.py:503
  4.7 0.6 copy-done.8
  5.6 0.6 fusion.6
  6.1 0.6 compare_select_fusion
  6.8 0.6 slice.48
  7.4 0.6 compare_convert_fusion
  8.0 0.8 %multiply_reduce_fusion = (f32[12]{0:T(128)S(1)}, f32[12]{0:T(128)S(1)}) fusion(f32[12,128]{1,0:T(8,128)S(1)} %bitcast.24, f32[1]{0:T(128)} %slice.48), kind=kLoop, calls=%fused_computation.13 | loop fusion | flops 12 | bytes 148 | tf_op jit(solution)/shard_map/slice | solution.py:506
  9.0 0.2 slice_reduce_fusion
  9.3 0.1 and_select_fusion.1.same_ref
  9.4 0.1 copy.34.cum_t_ref
  9.5 0.2 and_select_fusion.bias_ref
  9.7 0.2 copy.32
  9.9 0.7 copy-done.1
  10.7 0.2 copy.30.leave_ref
  10.9 0.7 copy-done.2
  11.7 0.7 copy-done.3
  12.4 0.3 convolution_bitcast_fusion.1
  12.7 0.5 copy-done.4
  13.2 0.3 convolution_bitcast_fusion
  13.6 0.8 copy-done.5
  14.4 0.1 copy-done.6
  14.5 0.1 copy-done.7
  14.6 63.8 %shard_map.153 = (bf16[128,768]{1,0:T(8,128)(2,1)S(1)}, bf16[128,768]{1,0:T(8,128)(2,1)S(1)}, bf16[128,768]{1,0:T(8,128)(2,1)S(1)}, f32[128,768]{1,0:T(8,128)S(1...) custom-call(bf16[128,768]{1,0:T(8,128)(2,1)S(1)} %copy-done.5, ...), custom_call_target="tpu_custom_call" | custom-call | flops 10000000000 | bytes 30000000 | tf_op jit(solution)/shard_map/pallas_call | solution.py:516
  78.3 2.1 %shard_map.154 = (bf16[128,768]{1,0:T(8,128)(2,1)}, bf16[128,128]{1,0:T(8,128)(2,1)}, bf16[128,128]{1,0:T(8,128)(2,1)}, f32[128,128]{1,0:T(8,128)S(1)}) custom-call(f32[2,128,768]{2,1,0:T(8,128)S(1)} %get-tuple-element.22.states_ref, bf16[128,768]{1,0:T(8,128)(2,1)S(1)} %multiply_convert_fusion.1.xl_ref, bf16[128,768]{1,0:T(8,128)(2,1)S(1)} %multiply_convert_fusion.de_ref, ...), custom_call_target="tpu_custom_call" | custom-call | tf_op jit(solution)/shard_map/pallas_call | solution.py:569
  80.4 0.7 copy.36
  81.1 0.7 copy.42
  81.7 0.7 copy.43
  82.4 0.7 copy.44
  (28 shorter events, 0.7 us)
Async XLA Ops:
  0.6 0.8 copy-start
  0.7 0.7 copy-start.9
  4.7 0.7 copy-start.8
  9.7 0.9 %copy-start.1 = (bf16[128,768]{1,0:T(8,128)(2,1)S(1)}, bf16[128,768]{1,0:T(8,128)(2,1)}, u32[]{:S(2)}) copy-start(bf16[128,768]{1,0:T(8,128)(2,1)} %do_ref.1) | copy-start | bytes 589828
  10.7 0.9 %copy-start.2 = (bf16[128,768]{1,0:T(8,128)(2,1)S(1)}, bf16[128,768]{1,0:T(8,128)(2,1)}, u32[]{:S(2)}) copy-start(bf16[128,768]{1,0:T(8,128)(2,1)} %x_ref.1) | copy-start | bytes 589828
  11.7 0.8 copy-start.3
  12.4 0.8 copy-start.4
  13.4 0.9 %copy-start.5 = (bf16[128,768]{1,0:T(8,128)(2,1)S(1)}, bf16[128,768]{1,0:T(8,128)(2,1)}, u32[]{:S(2)}) copy-start(bf16[128,768]{1,0:T(8,128)(2,1)} %q_ref.1) | copy-start | bytes 589828
  13.5 1.0 %copy-start.6 = (bf16[128,768]{1,0:T(8,128)(2,1)S(1)}, bf16[128,768]{1,0:T(8,128)(2,1)}, u32[]{:S(2)}) copy-start(bf16[128,768]{1,0:T(8,128)(2,1)} %k_ref.1) | copy-start | bytes 589828
  13.5 1.1 %copy-start.7 = (bf16[128,768]{1,0:T(8,128)(2,1)S(1)}, bf16[128,768]{1,0:T(8,128)(2,1)}, u32[]{:S(2)}) copy-start(bf16[128,768]{1,0:T(8,128)(2,1)} %v_ref.1) | copy-start | bytes 589828
